TPU v7x, 32 devices: a whole 2x2x4 slice. The times are simulated.
32 devices in a mesh: dp: 16 (over z, y, x), tensor: 2 (over core).
Axes of the slice: x: 2, y: 2, z: 4, core: 2. Of those that a mesh axis runs over, the one named last changes fastest.
Arguments:
- tokens: bfloat16 [32768, 768], P('dp', 'tensor'), may hold values from -6 to 6
- qkv_weight: bfloat16 [3, 768, 768], P(None, None, 'tensor'), may hold values from -0.21875 to 0.21875
- qv_bias: float32 [2, 768], P(None, 'tensor'), may hold values from -1.75 to 1.75
- out_weight: bfloat16 [768, 768], P('tensor'), may hold values from -0.875 to 0.875
- out_bias: float32 [768], P('tensor'), may hold values from -1.75 to 1.75
- first_gain: float32 [768], P('tensor'), may hold values from 0.25 to 1.75
- first_shift: float32 [768], P('tensor'), may hold values from -1.75 to 1.75
- up_weight: bfloat16 [768, 3072], P(None, 'tensor'), may hold values from -0.21875 to 0.21875
- up_bias: float32 [3072], P('tensor'), may hold values from -1.75 to 1.75
- down_weight: bfloat16 [3072, 768], P('tensor'), may hold values from -0.109375 to 0.109375
- down_bias: float32 [768], P('tensor'), may hold values from -1.75 to 1.75
- second_gain: float32 [768], P('tensor'), may hold values from 0.25 to 1.75
- second_shift: float32 [768], P('tensor'), may hold values from -1.75 to 1.75
- pool_weight: bfloat16 [768, 768], P('tensor'), may hold values from -0.21875 to 0.21875
- pool_bias: float32 [768], replicated, may hold values from -1.75 to 1.75
- log_temp: float32 [1], replicated, may hold values from -4.2 to -3.6
- segments: int32 [32, 1024], P('dp'), may hold values from 0 to 15, never falling along the last dimension, each value on 1 to 256 neighbouring positions
- cls_pos: int32 [32, 8], P('dp'), may hold values from 0 to 1023
- pair_index: int32 [256], P('dp'), may hold values from 0 to 255, each once
- attn_keep: int32 [32768, 768], P('dp', 'tensor'), may hold values 0 or 1
- ffn_keep: int32 [32768, 768], P('dp', 'tensor'), may hold values 0 or 1
- grad_out: bfloat16 [32768, 768], P('dp', 'tensor'), may hold values from -6 to 6
Outputs:
- layer_out: bfloat16 [32768, 768], P('dp', 'tensor')
- loss: float32 [1], replicated
- grad_tokens: float32 [32768, 768], P('dp', 'tensor')
- grad_qkv_weight: float32 [3, 768, 768], P(None, None, 'tensor')
- grad_qv_bias: float32 [2, 768], P(None, 'tensor')
- grad_out_weight: float32 [768, 768], P('tensor')
- grad_out_bias: float32 [768], P('tensor')
- grad_first_gain: float32 [768], P('tensor')
- grad_first_shift: float32 [768], P('tensor')
- grad_up_weight: float32 [768, 3072], P(None, 'tensor')
- grad_up_bias: float32 [3072], P('tensor')
- grad_down_weight: float32 [3072, 768], P('tensor')
- grad_down_bias: float32 [768], P('tensor')
- grad_second_gain: float32 [768], P('tensor')
- grad_second_shift: float32 [768], P('tensor')
- grad_pool_weight: float32 [768, 768], P('tensor')
- grad_pool_bias: float32 [768], replicated
- grad_log_temp: float32 [1], replicated
Inputs may be any that keep to these rules, and one draw needn't show every extreme that they name: `segments`: segment numbers never fall along a packed row; a segment holds 1 to 256 positions. `pair_index`: every pooled row is named by exactly one row.
All inputs are finite; a program needn't handle non-finite values. No bound on the sum of `attn_keep` or of `ffn_keep` on one device may be relied on, other than what follows from the above.
Results may differ from a plain program's by a relative error of at most 0.015.
Values may be sent and summed in bfloat16 or wider, within the bound.
No kernel may reach another device: no remote copies, remote signals or barrier semaphores. Data moves between devices by JAX's collectives and lax.ppermute only.
A program may use at most 192 MiB of HBM per device.

v0:
```python
import functools
import jax
import jax.numpy as jnp
from jax import lax
from jax.experimental import pallas as pl
from jax.experimental.pallas import tpu as pltpu
from jax.sharding import PartitionSpec as P

D = 768
HEAD_DIM = 64
PAIR = 2 * HEAD_DIM
BLOCK = 256
QROWS = 128
WIDE = QROWS + 512
NEAR = QROWS + 256
SWAP = [(0, 1), (1, 0)]
highest = lax.Precision.HIGHEST
f32 = jnp.float32
bf16 = jnp.bfloat16


def dot_nt(a, b, **kw):
    return lax.dot_general(a, b, (((1,), (1,)), ((), ())), preferred_element_type=f32, **kw)


def dot_tn(a, b):
    return lax.dot_general(a, b, (((0,), (0,)), ((), ())), preferred_element_type=f32)


def dot_nn(a, b):
    return jnp.dot(a, b, preferred_element_type=f32)


ORDER = []

MICROS = {
    "their_rows": 2, "both_rows": 2, "vectors": 1, "qkv": 5, "pooled": 9, "attend": 11, "ffn": 25, "contrast": 6, "down_back": 9,
    "down_own": 3.5, "up_back": 10, "up_own": 10, "out_back": 9, "attend_back": 21, "qkv_last": 4,
    "tokens_back": 5, "last_halves": 2, "stage": 1, "up_end": 3, "last_end": 3, "down_end": 3,
}


def norm(v):
    center = v - jnp.mean(v, axis=-1, keepdims=True)
    inv = lax.rsqrt(jnp.mean(center * center, axis=-1, keepdims=True) + 1e-06)
    return center * inv, inv


def norm_back(upstream, unit, inv, gain):
    scaled = upstream * gain
    return inv * (
        scaled
        - jnp.mean(scaled, axis=-1, keepdims=True)
        - unit * jnp.mean(scaled * unit, axis=-1, keepdims=True)
    )


def gelu_both(x):
    phi = 0.5 * (1.0 + lax.erf(x * (0.5 ** 0.5)))
    bell = jnp.exp(-0.5 * x * x) * 0.3989422804014327
    return x * phi, phi + x * bell


def lanes_of(me, half):
    return pl.ds(pl.multiple_of(me * half, 128), half)


def call(kernel, name, grid, scalars, ins, outs, scratch=(), vmem=26, after=(), aliases=None, free=False):
    after = [*after, *([] if free else ORDER[-1:])]
    n_scalars, n_ins, n_after = len(scalars), len(ins), len(after)

    def body(*refs):
        cut = n_scalars + n_ins
        kernel(*refs[:cut], *refs[cut + n_after :])

    def spec(shape, block, index):
        if block is None:
            zeros = (0,) * len(shape)
            return pl.BlockSpec(shape, lambda *a: zeros)
        return pl.BlockSpec(block, index)

    arrays = [a if b is None else pltpu.with_memory_space_constraint(a, pltpu.HBM) for a, b, _ in ins]
    result = pl.pallas_call(
        body,
        grid_spec=pltpu.PrefetchScalarGridSpec(
            num_scalar_prefetch=len(scalars),
            grid=grid,
            in_specs=[spec(a.shape, b, i) for a, b, i in ins]
            + [pl.BlockSpec(memory_space=pl.ANY)] * n_after,
            out_specs=[spec(s, b, i) for s, _, b, i in outs],
            scratch_shapes=list(scratch),
        ),
        out_shape=[jax.ShapeDtypeStruct(s, d) for s, d, _, _ in outs],
        compiler_params=pltpu.CompilerParams(vmem_limit_bytes=vmem << 20),
        cost_estimate=pl.CostEstimate(flops=int(MICROS[name] * 1.15e9), bytes_accessed=1000, transcendentals=0),
        input_output_aliases={n_scalars + i: o for i, o in (aliases or {}).items()},
        name=name,
    )(*scalars, *arrays, *after)
    if not free:
        ORDER.append(min(result, key=lambda r: r.size))
    return result


def put_halves(buf, me, mine, theirs):
    half = mine.shape[1]
    buf[:, lanes_of(me, half)] = mine.astype(buf.dtype)
    buf[:, lanes_of(1 - me, half)] = theirs.astype(buf.dtype)


def rows_kernel(me_ref, *refs):
    for i, o in zip(refs[: len(refs) // 2], refs[len(refs) // 2 :]):
        o[...] = i[...].astype(bf16)


def their_rows(me, arrays, length, after=()):
    half = arrays[0].shape[1]
    steps = length // 256
    return call(
        rows_kernel, "their_rows", (steps,), [me],
        [(a, (256, half), lambda i, m: ((1 - m[0]) * steps + i, 0)) for a in arrays],
        [((length, half), bf16, (256, half), lambda i, m: (i, 0))] * len(arrays),
        after=after,
    )


def both_rows_kernel(me_ref, mine, theirs, out):
    own = pl.program_id(0) // 2 == me_ref[0]

    @pl.when(own)
    def _():
        out[...] = mine[...]

    @pl.when(jnp.logical_not(own))
    def _():
        out[...] = theirs[...]


def both_rows(me, mine, theirs):
    length, half = mine.shape
    block = (length // 2, half)
    turn = lambda i, m: (i % 2, 0)
    return call(
        both_rows_kernel, "both_rows", (4,), [me], [(mine, block, turn), (theirs, block, turn)],
        [((2 * length, half), mine.dtype, block, lambda i, m: (i, 0))],
        free=True,
    )[0]


def vectors_kernel(units, me_ref, mine, theirs, qv_ref, up_ref, feats_ref):
    half = qv_ref.shape[1] // 2
    feats_ref[...] = jnp.zeros_like(feats_ref)
    for side, vec in enumerate((mine, theirs)):
        for row in range(2):
            qv_ref[row : row + 1, side * half : side * half + half] = vec[:, row * half : row * half + half]
        up_ref[:, side * units : side * units + units] = vec[:, 2 * half : 2 * half + units]
        spot = lanes_of(me_ref[0] if side == 0 else 1 - me_ref[0], half)
        for row in range(6):
            low = 2 * half + units + row * half
            feats_ref[row : row + 1, spot] = vec[:, low : low + half]


def vectors(me, mine, theirs, units, half):
    return call(
        functools.partial(vectors_kernel, units), "vectors", (1,), [me],
        [(mine, None, None), (theirs, None, None)],
        [((2, 2 * half), f32, None, None), ((1, 2 * units), f32, None, None), ((8, 2 * half), f32, None, None)],
    )


def qkv_kernel(me_ref, mine, theirs, w_here, w_there, bias, x_ref, q_ref, k_ref, v_ref):
    put_halves(x_ref, me_ref[0], mine[...], theirs[...])
    half = mine.shape[1]
    for c, out in enumerate((q_ref, k_ref, v_ref)):
        for side, w in enumerate((w_here, w_there)):
            cols = slice(side * half, side * half + half)
            y = dot_nn(x_ref[...], w[c])
            if c != 1:
                y = y + bias[c // 2 : c // 2 + 1, cols]
            out[:, cols] = y.astype(bf16)


def project(me, tokens, x_there, w_here, w_there, bias, length):
    half = tokens.shape[1]
    rows = 512
    steps = length // rows
    band = (rows, 2 * half)
    return call(
        qkv_kernel, "qkv", (steps,), [me],
        [
            (tokens, (rows, half), lambda i, m: (m[0] * steps + i, 0)),
            (x_there, (rows, half), lambda i, m: (i, 0)),
            (w_here, None, None),
            (w_there, None, None),
            (bias, None, None),
        ],
        [((length, 2 * half), bf16, band, lambda i, m: (i, 0))] * 4,
    )


def window_paths(step, length, seg_ref, run):
    first = step * QROWS
    near = pl.multiple_of(jnp.clip(first - 128, 0, length - NEAR), 128)
    left = seg_ref[jnp.maximum(near - 1, 0)] == seg_ref[first]
    right = seg_ref[jnp.minimum(near + NEAR, length - 1)] == seg_ref[first + QROWS - 1]
    spills = jnp.logical_or(
        jnp.logical_and(near > 0, left), jnp.logical_and(near + NEAR < length, right)
    )
    far = pl.multiple_of(jnp.clip(first - 256, 0, length - WIDE), 128)

    @pl.when(jnp.logical_not(spills))
    def _():
        run(NEAR, near)

    @pl.when(spills)
    def _():
        run(WIDE, far)


def fill_bias(bias_ref, col_ref, row_ref, width, start):
    bias = jnp.where(col_ref[pl.ds(start, width), :] == row_ref[...], 0.0, -1e30)
    for n in range(bias_ref.shape[1] // QROWS):
        bias_ref[0:width, n * QROWS : (n + 1) * QROWS] = bias


def head_mask(h):
    lane = lax.broadcasted_iota(jnp.int32, (1, PAIR), 1)
    return (lane // HEAD_DIM == h).astype(bf16)


def attend_kernel(length, pairs, seg_ref, col_ref, row_ref, q_ref, k_ref, v_ref, ctx_ref, lse_ref, bias_ref):
    def run(width, start):
        fill_bias(bias_ref, col_ref, row_ref, width, start)
        rows = pl.ds(start, width)
        for j in range(pairs):
            lanes = slice(j * PAIR, j * PAIR + PAIR)
            q2 = q_ref[:, lanes] * bf16(HEAD_DIM ** (-0.5))
            keys = k_ref[rows, lanes]
            values = v_ref[rows, lanes]
            parts = []
            for h in range(2):
                scores = dot_nt(keys, q2 * head_mask(h)) + bias_ref[0:width, :]
                top = jnp.max(scores, axis=0, keepdims=True)
                expo = jnp.exp(scores - top)
                total = jnp.sum(expo, axis=0, keepdims=True)
                out = dot_tn(values, expo.astype(bf16))[h * HEAD_DIM : (h + 1) * HEAD_DIM]
                parts.append(out * (1.0 / total))
                lse_ref[8 * h + j : 8 * h + j + 1, :] = top + jnp.log(total)
            ctx_ref[:, lanes] = jnp.concatenate(parts, axis=0).T.astype(bf16)

    window_paths(pl.program_id(0), length, seg_ref, run)


def attend(seg, col, q, k, v, after):
    length, width = q.shape
    band = lambda i, s: (i, 0)
    block = (QROWS, width)
    return call(
        functools.partial(attend_kernel, length, width // PAIR), "attend", (length // QROWS,),
        [seg.reshape(length)],
        [
            (col, None, None),
            (seg.reshape(1, length), (1, QROWS), lambda i, s: (0, i)),
            (q, block, band),
            (k, None, None),
            (v, None, None),
        ],
        [
            ((length, width), bf16, block, band),
            ((16, length), f32, (16, QROWS), lambda i, s: (0, i)),
        ],
        [pltpu.VMEM((WIDE, QROWS), f32)],
        after=after,
    )


def attend_back_kernel(
    length, chosen, seg_ref, col_ref, row_ref, q_ref, k_ref, v_ref, do_ref, lse_ref, delta_ref,
    dq_ref, dk_ref, dv_ref, bias_ref, dk_acc, dv_acc,
):
    step = pl.program_id(0)

    @pl.when(step == 0)
    def _():
        dk_acc[...] = jnp.zeros_like(dk_acc)
        dv_acc[...] = jnp.zeros_like(dv_acc)

    def both(ref, j):
        return jnp.concatenate([ref[j : j + 1, :], ref[8 + j : 9 + j, :]], axis=1)

    def run(width, start):
        fill_bias(bias_ref, col_ref, row_ref, width, start)
        rows = pl.ds(start, width)
        for n, j in enumerate(chosen):
            lanes = slice(j * PAIR, j * PAIR + PAIR)
            slot = slice(n * PAIR, n * PAIR + PAIR)
            q2 = q_ref[:, lanes] * bf16(HEAD_DIM ** (-0.5))
            do2 = do_ref[:, lanes]
            keys = k_ref[rows, lanes]
            values = v_ref[rows, lanes]
            queries = jnp.concatenate([q2 * head_mask(0), q2 * head_mask(1)], axis=0)
            grads = jnp.concatenate([do2 * head_mask(0), do2 * head_mask(1)], axis=0)
            scores = dot_nt(keys, queries) + bias_ref[0:width, :]
            probs = jnp.exp(scores - both(lse_ref, j))
            grad_probs = dot_nt(values, grads)
            grad_scores = (probs * (grad_probs - both(delta_ref, j))).astype(bf16)
            dv_acc[rows, slot] += dot_nn(probs.astype(bf16), grads)
            dk_acc[rows, slot] += dot_nn(grad_scores, queries)
            dq = dot_tn(keys, grad_scores)
            dq = jnp.concatenate([dq[:HEAD_DIM, :QROWS], dq[HEAD_DIM:, QROWS:]], axis=0).T
            dq_ref[:, slot] = (dq * (HEAD_DIM ** (-0.5))).astype(bf16)

    window_paths(step, length, seg_ref, run)

    @pl.when(step == length // QROWS - 1)
    def _():
        dk_ref[...] = dk_acc[...].astype(bf16)
        dv_ref[...] = dv_acc[...].astype(bf16)


def attend_back(seg, col, q, k, v, grad_ctx, lse, delta, chosen, after):
    length, width = q.shape
    cols = len(chosen) * PAIR
    block = (QROWS, width)
    band = lambda i, s: (i, 0)
    flat = lambda i, s: (0, i)
    whole = ((length, cols), bf16, None, None)
    return call(
        functools.partial(attend_back_kernel, length, chosen), "attend_back", (length // QROWS,),
        [seg.reshape(length)],
        [
            (col, None, None),
            (seg.reshape(1, length), (1, QROWS), flat),
            (q, block, band),
            (k, None, None),
            (v, None, None),
            (grad_ctx, block, band),
            (lse, (16, QROWS), flat),
            (delta, (16, QROWS), flat),
        ],
        [((length, cols), bf16, (QROWS, cols), band), whole, whole],
        [
            pltpu.VMEM((WIDE, 2 * QROWS), f32),
            pltpu.VMEM((length, cols), f32),
            pltpu.VMEM((length, cols), f32),
        ],
        after=after,
    )


UNITS = 512
FROWS = 512


def sides(sides_count, step, here_first, run_here, run_there):
    low, high = (run_here, run_there) if here_first else (run_there, run_here)

    @pl.when(step < sides_count)
    def _():
        low()

    @pl.when(step >= sides_count)
    def _():
        high()


def ffn_kernel(
    count, me_ref, cls_ref, pair_ref, ctx_ref, x_ref, ow_here, ow_there, keep1_mine, keep1_theirs, uw_here, uw_there, dw_here,
    dw_there, up_b, feats, keep_mine, keep_theirs, res_ref, low_ref, act_ref, slope_ref, mixed_ref, mine_ref,
    theirs_ref, pooled_ref, keep, value_buf,
):
    step = pl.program_id(0)
    length = low_ref.shape[0]

    @pl.when(step == 0)
    def _():
        mixed_ref[...] = jnp.zeros_like(mixed_ref)
        side = ow_here.shape[0]
        for r in range(length // BLOCK):
            rows = slice(r * BLOCK, (r + 1) * BLOCK)
            put_halves(keep, me_ref[0], keep1_mine[rows, :].astype(f32), keep1_theirs[rows, :])
            branch = dot_nn(ctx_ref[rows, :side], ow_here[...]) + dot_nn(ctx_ref[rows, side:], ow_there[...])
            residual = x_ref[rows, :].astype(f32) + (branch + feats[0:1, :]) * (keep[...] * (1 / 0.9))
            res_ref[rows, :] = residual
            low_ref[rows, :] = (norm(residual)[0] * feats[1:2, :] + feats[2:3, :]).astype(bf16)

    def run(up, down):
        def go():
            for r in range(length // FROWS):
                rows = slice(r * FROWS, (r + 1) * FROWS)
                pre = dot_nn(low_ref[rows, :], up[...]) + up_b[...]
                value, slope = gelu_both(pre)
                value = value.astype(bf16)
                act_ref[rows, :] = value
                slope_ref[rows, :] = slope.astype(bf16)
                mixed_ref[rows, :] += dot_nn(value, down[...])

        return go

    sides(count, step, True, run(uw_here, dw_here), run(uw_there, dw_there))

    @pl.when(step == 2 * count - 1)
    def _():
        half = mine_ref.shape[1]
        me = me_ref[0]
        width = value_buf.shape[1]
        chosen = cls_ref.shape[0]
        line = lax.broadcasted_iota(jnp.int32, (16, BLOCK), 0)
        spot = jnp.full((16, BLOCK), -1, jnp.int32)
        for c in range(chosen):
            spot = jnp.where(line == c, cls_ref[c], spot)
        line = lax.broadcasted_iota(jnp.int32, (16, width), 0)
        lane = lax.broadcasted_iota(jnp.int32, (16, width), 1)
        numbers = jnp.zeros((16, width), jnp.int32)
        for c in range(chosen):
            number = pair_ref[me * chosen + c]
            numbers = jnp.where((lane == c) & (line == chosen), number // 64, numbers)
            numbers = jnp.where((lane == c) & (line == chosen + 1), number % 64, numbers)
        pooled = numbers.astype(f32)
        for r in range(length // BLOCK):
            rows = slice(r * BLOCK, (r + 1) * BLOCK)
            put_halves(keep, me, keep_mine[rows, :].astype(f32), keep_theirs[rows, :])
            hidden = norm(res_ref[rows, :])[0] * feats[1:2, :] + feats[2:3, :]
            mixed = hidden + (mixed_ref[rows, :] + feats[3:4, :]) * (keep[...] * (1 / 0.9))
            mixed_ref[rows, :] = mixed
            value_buf[...] = (norm(mixed)[0] * feats[4:5, :] + feats[5:6, :]).astype(bf16)
            here = lax.broadcasted_iota(jnp.int32, (16, BLOCK), 1) + r * BLOCK
            pooled = pooled + dot_nn((here == spot).astype(bf16), value_buf[...])
            mine_ref[rows, :] = value_buf[:, lanes_of(me, half)]
            theirs_ref[rows, :] = value_buf[:, lanes_of(1 - me, half)]
        pooled_ref[...] = pooled.astype(bf16)


def feed_forward(me, cls, pair_index, ctx, x, ow_here, ow_there, keep1, uw_here, uw_there, dw_here, dw_there, up_b, feats, keep):
    length, width = x.shape
    half = width // 2
    count = uw_here.shape[1] // UNITS
    units = 2 * uw_here.shape[1]
    first = lambda i: jnp.minimum(i, count - 1)
    second = lambda i: jnp.maximum(i - count, 0)
    return call(
        functools.partial(ffn_kernel, count), "ffn", (2 * count,), [me, cls, pair_index],
        [
            (ctx, None, None),
            (x, None, None),
            (ow_here, None, None),
            (ow_there, None, None),
            (keep1[0], (length, half), lambda i, m, c, p: (m[0], 0)),
            (keep1[1], None, None),
            (uw_here, (width, UNITS), lambda i, m, c, p: (0, first(i))),
            (uw_there, (width, UNITS), lambda i, m, c, p: (0, second(i))),
            (dw_here, (UNITS, width), lambda i, m, c, p: (first(i), 0)),
            (dw_there, (UNITS, width), lambda i, m, c, p: (second(i), 0)),
            (up_b, (1, UNITS), lambda i, m, c, p: (0, i)),
            (feats, None, None),
            (keep[0], (length, half), lambda i, m, c, p: (m[0], 0)),
            (keep[1], None, None),
        ],
        [
            ((length, width), f32, None, None),
            ((length, width), bf16, None, None),
            ((length, units), bf16, (length, UNITS), lambda i, m, c, p: (0, i)),
            ((length, units), bf16, (length, UNITS), lambda i, m, c, p: (0, i)),
            ((length, width), f32, None, None),
            ((length, half), bf16, None, None),
            ((length, half), bf16, None, None),
            ((16, width), bf16, None, None),
        ],
        [pltpu.VMEM((BLOCK, width), f32), pltpu.VMEM((BLOCK, width), bf16)],
        vmem=36,
    )


def down_back_kernel(
    me_ref, cls_ref, mixed_ref, go_mine, go_theirs, pooled_ref, feats, keep_mine, keep_theirs, act_ref,
    g_ref, gm_ref, sums_ref, there_ref, buf, keep,
):
    length, width = mixed_ref.shape

    @pl.when(pl.program_id(0) == 0)
    def _():
        me = me_ref[0]
        put_halves(buf, me, go_mine[...].astype(f32), go_theirs[...])
        for c in range(cls_ref.shape[0]):
            spot = pl.ds(cls_ref[c], 1)
            buf[spot, :] = buf[spot, :] + pooled_ref[c : c + 1, :]
        gain_sum = jnp.zeros((1, width), f32)
        shift_sum = jnp.zeros((1, width), f32)
        bias_sum = jnp.zeros((1, width), f32)
        for r in range(length // BLOCK):
            rows = slice(r * BLOCK, (r + 1) * BLOCK)
            upstream = buf[rows, :]
            unit, inv = norm(mixed_ref[rows, :])
            back = norm_back(upstream, unit, inv, feats[4:5, :])
            gm_ref[rows, :] = back
            put_halves(keep, me, keep_mine[rows, :].astype(f32), keep_theirs[rows, :])
            g = (back * (keep[...] * (1 / 0.9))).astype(bf16)
            g_ref[rows, :] = g
            gain_sum = gain_sum + jnp.sum(upstream * unit, axis=0, keepdims=True)
            shift_sum = shift_sum + jnp.sum(upstream, axis=0, keepdims=True)
            bias_sum = bias_sum + jnp.sum(g.astype(f32), axis=0, keepdims=True)
        sums_ref[...] = jnp.concatenate(
            [bias_sum, gain_sum, shift_sum, jnp.zeros((5, width), f32)], axis=0
        )

    there_ref[...] = dot_tn(act_ref[...], g_ref[...]).astype(bf16)


def down_back(me, cls, mixed, go_arg, go_there, grad_pooled, feats, keep, act):
    length, width = mixed.shape
    half = width // 2
    units = act.shape[1] // 2
    count = units // UNITS
    part = lambda a: (a, (length, half), lambda i, m, c: (m[0], 0))
    return call(
        down_back_kernel, "down_back", (count,), [me, cls],
        [
            (mixed, None, None),
            part(go_arg),
            (go_there, None, None),
            (grad_pooled, None, None),
            (feats, None, None),
            part(keep[0]),
            (keep[1], None, None),
            (act, (length, UNITS), lambda i, m, c: (0, i + count)),
        ],
        [
            ((length, width), bf16, None, None),
            ((length, width), f32, None, None),
            ((8, width), f32, None, None),
            ((units, width), bf16, (UNITS, width), lambda i, m, c: (i, 0)),
        ],
        [pltpu.VMEM((length, width), f32), pltpu.VMEM((BLOCK, width), f32)],
    )


def down_own_kernel(bit_ref, act_ref, g_ref, got_ref, keep_ref, send_ref):
    grad = (dot_tn(act_ref[...], g_ref[...]) + got_ref[...].astype(f32)).astype(bf16)
    mine = pl.program_id(0) == bit_ref[0]

    @pl.when(mine)
    def _():
        keep_ref[...] = grad

    @pl.when(jnp.logical_not(mine))
    def _():
        send_ref[...] = grad


def down_own(bit, act, g, got):
    length, width = g.shape
    rows = got.shape[0] // 2
    return call(
        down_own_kernel, "down_own", (2,), [bit],
        [
            (act, (length, rows), lambda i, s: (0, i)),
            (g, None, None),
            (got, (rows, width), lambda i, s: (i, 0)),
        ],
        [((rows, width), bf16, None, None)] * 2,
    )


def up_back_kernel(
    own, bit_ref, low_ref, g_ref, slope_ref, up, down, *refs,
):
    if own:
        start_ref, got_ref, part_ref, bias_ref, *out_refs, grad_buf = refs
    else:
        part_ref, bias_ref, out_ref = refs
    step = pl.program_id(0)
    length, width = g_ref.shape

    @pl.when(step == 0)
    def _():
        part_ref[...] = start_ref[...] if own else jnp.zeros_like(part_ref)

    total = jnp.zeros((1, UNITS), f32)
    grads = []
    for r in range(length // FROWS):
        rows = slice(r * FROWS, (r + 1) * FROWS)
        gu = (dot_nt(g_ref[rows, :], down[...]) * slope_ref[rows, :].astype(f32)).astype(bf16)
        total = total + jnp.sum(gu.astype(f32), axis=0, keepdims=True)
        part_ref[rows, :] += dot_nt(gu, up[...])
        grads.append(gu)
    bias_ref[...] = total
    grad = dot_tn(low_ref[...], jnp.concatenate(grads, axis=0))
    if own:
        grad_buf[...] = (grad + got_ref[...].astype(f32)).astype(bf16)
        halves_out(bit_ref[0], grad_buf, out_refs)
    else:
        out_ref[...] = grad.astype(bf16)


def up_back(bit, low, g, slope, up, down, own, start=None, got=None, after=()):
    length, width = g.shape
    units = up.shape[1]
    count = units // UNITS
    skip = 0 if own else count
    ins = [
        (low, None, None),
        (g, None, None),
        (slope, (length, UNITS), lambda i, s: (0, i + skip)),
        (up, (width, UNITS), lambda i, s: (0, i)),
        (down, (UNITS, width), lambda i, s: (i, 0)),
    ]
    rows = width // 2 if own else width
    outs = [
        ((length, width), f32, None, None),
        ((1, units), f32, (1, UNITS), lambda i, s: (0, i)),
    ] + [((rows, units), bf16, (rows, UNITS), lambda i, s: (0, i))] * (width // rows)
    scratch = []
    if own:
        scratch = [pltpu.VMEM((width, UNITS), bf16)]
        ins += [(start, None, None), (got, (width, UNITS), lambda i, s: (0, i))]
    return call(
        functools.partial(up_back_kernel, own), "up_own" if own else "up_back", (count,), [bit], ins, outs, scratch,
        after=after,
    )


def out_back_kernel(
    me_ref, gm_ref, part_ref, res_ref, ctx_ref, keep_mine, keep_theirs, w_here, w_there, feats,
    gr_ref, gc_ref, delta_ref, sums_ref, there_ref, here_ref, keep, acc, sums,
):
    step = pl.program_id(0)
    width = gm_ref.shape[1]
    half = width // 2
    rows = pl.ds(pl.multiple_of(step * BLOCK, BLOCK), BLOCK)
    unit, inv = norm(res_ref[rows, :])
    upstream = gm_ref[rows, :] + part_ref[rows, :]
    back = norm_back(upstream, unit, inv, feats[1:2, :])
    gr_ref[...] = back
    put_halves(keep, me_ref[0], keep_mine[...].astype(f32), keep_theirs[...])
    g = (back * (keep[...] * (1 / 0.9))).astype(bf16)
    gc_ref[:, :half] = dot_nt(g, w_here[...]).astype(bf16)
    gc_ref[:, half:] = dot_nt(g, w_there[...]).astype(bf16)
    grad = dot_tn(ctx_ref[...], g)
    prod = gc_ref[...].astype(f32) * ctx_ref[...].astype(f32)
    high = prod.astype(bf16)
    rest = (prod - high.astype(f32)).astype(bf16)
    row = lax.broadcasted_iota(jnp.int32, (16, width), 0)
    lane = lax.broadcasted_iota(jnp.int32, (16, width), 1)
    pick = (lane // HEAD_DIM == (row & 7) * 2 + (row >> 3)).astype(bf16)
    delta_ref[...] = dot_nt(pick, high) + dot_nt(pick, rest)
    parts = [
        jnp.sum(g.astype(f32), axis=0, keepdims=True),
        jnp.sum(upstream * unit, axis=0, keepdims=True),
        jnp.sum(upstream, axis=0, keepdims=True),
        jnp.zeros((5, width), f32),
    ]
    row = jnp.concatenate(parts, axis=0)

    @pl.when(step == 0)
    def _():
        acc[...] = grad
        sums[...] = row

    @pl.when(step > 0)
    def _():
        acc[...] += grad
        sums[...] += row

    @pl.when(step == pl.num_programs(0) - 1)
    def _():
        here_ref[...] = acc[:half, :].astype(bf16)
        there_ref[...] = acc[half:, :].astype(bf16)
        sums_ref[...] = sums[...]


def out_back(me, gm, part, res, ctx, keep, w_here, w_there, feats, after):
    length, width = gm.shape
    half = width // 2
    steps = length // BLOCK
    band = lambda i, m: (i, 0)
    block = (BLOCK, width)
    return call(
        out_back_kernel, "out_back", (steps,), [me],
        [
            (gm, None, None),
            (part, None, None),
            (res, None, None),
            (ctx, block, band),
            (keep[0], (BLOCK, half), lambda i, m: (m[0] * steps + i, 0)),
            (keep[1], (BLOCK, half), band),
            (w_here, None, None),
            (w_there, None, None),
            (feats, None, None),
        ],
        [
            ((length, width), f32, block, band),
            ((length, width), bf16, block, band),
            ((16, length), f32, (16, BLOCK), lambda i, m: (0, i)),
            ((8, width), f32, None, None),
            ((half, width), bf16, None, None),
            ((half, width), bf16, None, None),
        ],
        [pltpu.VMEM((BLOCK, width), f32), pltpu.VMEM((width, width), f32), pltpu.VMEM((8, width), f32)],
        after=after,
    )


def qkv_last_kernel(
    me_ref, x_ref, dq, dk, dv, bias_here, bias_there, sums1, sums2, there_ref, here_ref, vh, vt, both,
):
    width = x_ref.shape[1]
    half = width // 2
    sums = []
    for c, g in enumerate((dq, dk, dv)):
        grad = dot_tn(x_ref[...], g[...]).astype(bf16)
        here_ref[c * width : (c + 1) * width, :] = grad[:, :half]
        there_ref[c * width : (c + 1) * width, :] = grad[:, half:]
        if c != 1:
            sums.append(jnp.sum(g[...].astype(f32), axis=0, keepdims=True))
    vh[...] = jnp.zeros_like(vh)
    vt[...] = jnp.zeros_like(vt)
    for side, (v, bias) in enumerate(((vh, bias_here), (vt, bias_there))):
        for row in range(2):
            v[row : row + 1, :] = sums[row][:, side * half : side * half + half]
        at = 2
        for n in range(bias.shape[1] // half):
            v[at : at + 1, :] = bias[:, n * half : (n + 1) * half]
            at += 1
    both[0:8, :] = sums1[...]
    both[8:16, :] = sums2[...]
    for v, m in ((vh, me_ref[0]), (vt, 1 - me_ref[0])):
        v[at : at + 3, :] = both[0:3, lanes_of(m, half)]
        v[at + 3 : at + 6, :] = both[8:11, lanes_of(m, half)]
    low = 3 * width
    for v, ref in ((vh, here_ref), (vt, there_ref)):
        ref[low : low + 16, :] = v[...].astype(bf16)
        ref[low + 16 :, :] = jnp.zeros((ref.shape[0] - low - 16, half), bf16)


def qkv_last(me, x, grads, bias_here, bias_there, sums1, sums2):
    width = x.shape[1]
    half = width // 2
    return call(
        qkv_last_kernel, "qkv_last", (1,), [me],
        [(a, None, None) for a in (x, *grads, bias_here, bias_there, sums1, sums2)],
        [((3 * width + 128, half), bf16, None, None)] * 2,
        [pltpu.VMEM((16, half), f32), pltpu.VMEM((16, half), f32), pltpu.VMEM((16, width), f32)],
    )


def tokens_back_kernel(me_ref, gr_ref, dq, dk, dv, w_here, w_there, mine_ref, theirs_ref, buf):
    half = mine_ref.shape[1]
    total = gr_ref[...]
    rows = pl.ds(pl.multiple_of(pl.program_id(0) * 512, 512), 512)
    for c, g in enumerate((dq[...], dk[rows, :], dv[rows, :])):
        total = total + dot_nt(g[:, :half], w_here[c]) + dot_nt(g[:, half:], w_there[c])
    buf[...] = total
    mine_ref[...] = buf[:, lanes_of(me_ref[0], half)]
    theirs_ref[...] = buf[:, lanes_of(1 - me_ref[0], half)]


def tokens_back(me, gr, grads, w_here, w_there):
    length, width = gr.shape
    half = width // 2
    band = lambda i, m: (i, 0)
    return call(
        tokens_back_kernel, "tokens_back", (length // 512,), [me],
        [(a, (512, width), band) for a in (gr, grads[0])]
        + [(a, None, None) for a in (*grads[1:], w_here, w_there)],
        [((length, half), f32, (512, half), band)] * 2,
        [pltpu.VMEM((512, width), f32)],
    )


def other(x):
    return lax.ppermute(x, "tensor", SWAP)


def across(x, mask, size):
    return lax.ppermute(x, "dp", [(i, i ^ mask) for i in range(size)])


def halves_out(at, buf, outs, low=0):
    rows = outs[0].shape[0]
    for m, out in enumerate(outs):
        start = pl.multiple_of(low + (at ^ m) * rows, 8)
        out[...] = buf[pl.ds(start, rows), :].astype(bf16)


def last_halves_kernel(cuts, here_ref, gq_here, gq_got, go_here, go_got, *refs):
    *outs, buf = refs
    rows, cols = gq_here.shape
    buf[:rows, :] = gq_here[...].astype(f32) + gq_got[...].astype(f32)
    half = go_here.shape[0]
    for side in range(2):
        lanes = slice(side * cols, side * cols + cols)
        low = rows + side * half
        buf[low : low + half, :] = go_here[:, lanes].astype(f32) + go_got[:, lanes].astype(f32)
    low = 0
    for n, (high, bit) in enumerate(cuts):
        halves_out((here_ref[0] >> bit) & 1, buf, outs[2 * n : 2 * n + 2], low)
        low = high


def last_halves(here, gq_here, gq_got, go_here, go_got, cuts):
    rows, cols = gq_here.shape
    rows += 2 * go_here.shape[0]
    lows = [0] + [high for high, _ in cuts[:-1]]
    outs = call(
        functools.partial(last_halves_kernel, cuts), "last_halves", (1,), [here],
        [(x, None, None) for x in (gq_here, gq_got, go_here, go_got)],
        [(((high - low) // 2, cols), bf16, None, None) for low, (high, _) in zip(lows, cuts) for _ in range(2)],
        [pltpu.VMEM((rows, cols), f32)],
    )
    return [outs[2 * n : 2 * n + 2] for n in range(len(cuts))]


def sum_of(refs):
    total = refs[0][...].astype(f32)
    for a in refs[1:]:
        total = total + a[...].astype(f32)
    return total


def stage_kernel(jobs, here_ref, *refs):
    n_ins = sum(n for _, n, _, _ in jobs)
    n_outs = sum(2 if kind == "fold" else 1 for kind, _, _, _ in jobs)
    ins, outs, bufs = list(refs[:n_ins]), list(refs[n_ins : n_ins + n_outs]), list(refs[n_ins + n_outs :])
    for kind, n, bit, many in jobs:
        parts, ins = ins[:n], ins[n:]
        if kind == "total":
            outs.pop(0)[...] = sum_of(parts).astype(bf16)
            continue
        at = (here_ref[0] >> bit) & (many - 1)
        buf = bufs.pop(0)
        if kind == "fold":
            buf[...] = sum_of(parts)
            halves_out(at, buf, outs[:2])
            outs = outs[2:]
        else:
            place(buf, at, parts, 0)
            outs.pop(0)[...] = buf[...].astype(bf16)


def stage(here, *jobs, free=False):
    outs, scratch, counts = [], [], []
    for kind, parts, _ in jobs:
        rows, cols = parts[0].shape
        if kind == "fold":
            outs += [((rows // 2, cols), bf16, None, None)] * 2
            scratch.append(pltpu.VMEM((rows, cols), f32))
        elif kind == "total":
            outs.append(((rows, cols), bf16, None, None))
        else:
            outs.append(((len(parts) * rows, cols), bf16, None, None))
            scratch.append(pltpu.VMEM((len(parts) * rows, cols), f32))
        counts.append(2 if kind == "fold" else 1)
    results = call(
        functools.partial(stage_kernel, [(kind, len(parts), bit, len(parts)) for kind, parts, bit in jobs]), "stage",
        (1,), [here], [(p, None, None) for _, parts, _ in jobs for p in parts], outs, scratch, free=free,
    )
    split = []
    for n in counts:
        split.append(results[:n] if n > 1 else results[0])
        results = results[n:]
    return split


class Chain:
    def __init__(self, halves, order, size):
        self.order, self.size, self.step = order, size, 0
        self.parts = halves
        self.send(halves[1])

    def send(self, x):
        bit = self.order[self.step]
        self.parts = [self.parts[0], across(x, 1 << bit, self.size)]

    def job(self):
        last = len(self.order) - 1
        if self.step < last:
            return ("fold", self.parts, self.order[self.step + 1])
        if self.step == last:
            return ("total", self.parts, 0)
        return ("join", self.parts, self.order[2 * last + 1 - self.step])

    def take(self, result):
        last = len(self.order) - 1
        self.step += 1
        if self.step <= last:
            self.parts = result
            bit, x = self.order[self.step], result[1]
        else:
            self.parts = [result, result]
            bit, x = self.order[2 * last + 1 - self.step], result
        self.parts = [self.parts[0], across(x, 1 << bit, self.size)]


def advance(here, *chains, free=False):
    for chain, result in zip(chains, stage(here, *[c.job() for c in chains], free=free)):
        chain.take(result)


def plain_sum(at, halves):
    whole = jnp.where(at == 0, jnp.stack(halves), jnp.stack(halves[::-1]))
    whole = lax.psum(whole, "dp")
    return jnp.where(at == 0, whole, whole[::-1])


def place(buf, at, parts, low):
    rows = parts[0].shape[0]
    for m, q in enumerate(parts):
        buf[pl.ds(pl.multiple_of(low + (at ^ m) * rows, 8), rows), :] = q[...].astype(buf.dtype)


def end_kernel(at_ref, mine, theirs, out):
    mine_now = pl.program_id(0) // 2 == at_ref[0]
    rows = out.shape[0]
    low = pl.multiple_of(pl.program_id(0) % 2 * rows, 16)

    @pl.when(mine_now)
    def _():
        out[...] = mine[pl.ds(low, rows), :].astype(f32)

    @pl.when(jnp.logical_not(mine_now))
    def _():
        out[...] = theirs[pl.ds(low, rows), :].astype(f32)


def end(at, halves, name):
    rows, cols = halves[0].shape
    return call(
        end_kernel, name, (4,), [at], [(q, None, None) for q in halves],
        [((2 * rows, cols), f32, (rows // 2, cols), lambda i, s: (i, 0))],
        free=True,
    )[0]


def last_end_kernel(bits, here_ref, *refs):
    *halves, qkv_ref, vec_ref, out_ref, buf = refs
    low = 0
    for n, bit in enumerate(bits):
        place(buf, (here_ref[0] >> bit) & 1, halves[2 * n : 2 * n + 2], low)
        low += 2 * halves[2 * n].shape[0]
    rows, cols = qkv_ref.shape[1:]
    for c in range(3):
        qkv_ref[c] = buf[c * rows : (c + 1) * rows, :]
    vec_ref[...] = buf[3 * rows : 3 * rows + 16, :]
    half = out_ref.shape[0]
    low = buf.shape[0] - 2 * half
    for side in range(2):
        out_ref[:, side * cols : side * cols + cols] = buf[low + side * half : low + (side + 1) * half, :]


def last_end(here, bands, bits, half):
    rows = sum(2 * b[0].shape[0] for b in bands)
    cols = bands[0][0].shape[1]
    return call(
        functools.partial(last_end_kernel, bits), "last_end", (1,), [here], [(q, None, None) for b in bands for q in b],
        [((3, 2 * cols, cols), f32, None, None), ((16, cols), f32, None, None), ((half, 2 * cols), f32, None, None)],
        [pltpu.VMEM((rows, cols), f32)],
        free=True,
    )


def contrast(pooled_all, pool_w, pool_bias, log_temp, pairs_all):
    squash_float = jnp.tanh(dot_nn(pooled_all, pool_w) + pool_bias)
    squash = squash_float.astype(bf16).astype(f32)
    inv_norm = lax.rsqrt(jnp.sum(squash * squash, axis=-1, keepdims=True) + 1e-06)
    unit_all = squash * inv_norm
    temp = jnp.exp(-log_temp[0])
    logits = jnp.dot(unit_all, unit_all.T, precision=highest) * temp
    ids = jnp.arange(pooled_all.shape[0], dtype=jnp.int32)
    masked = jnp.where(ids[None, :] == ids[:, None], -1e30, logits)
    row_top = jnp.max(masked, axis=-1, keepdims=True)
    row_expo = jnp.exp(masked - row_top)
    row_total = jnp.sum(row_expo, axis=-1, keepdims=True)
    chosen = (ids[None, :] == pairs_all[:, None]).astype(f32)
    row_lse = row_top[:, 0] + jnp.log(row_total[:, 0])
    loss_total = jnp.sum(row_lse - jnp.sum(chosen * logits, axis=-1))
    grad_logits = row_expo / row_total - chosen
    grad_temp = -jnp.sum(grad_logits * logits)
    grad_unit = jnp.dot(grad_logits + grad_logits.T, unit_all, precision=highest) * temp
    grad_squash = inv_norm * (
        grad_unit - unit_all * jnp.sum(unit_all * grad_unit, axis=-1, keepdims=True)
    )
    grad_pool_pre = (grad_squash * (1.0 - squash_float * squash_float)).astype(bf16)
    return loss_total, grad_temp, grad_pool_pre


def contrast_kernel(
    count, rank_ref, me_ref, all_here, all_there, w_here, w_there, bias_ref, temp_ref, gw_ref, gb_ref,
    gp_ref, scalars_ref, all_ref, w_ref, pooled_ref, grad_ref,
):
    batch, width = pooled_ref.shape
    half = w_here.shape[0]
    me = me_ref[0]
    w_ref[pl.ds(pl.multiple_of(me * half, 128), half), :] = w_here[...]
    w_ref[pl.ds(pl.multiple_of((1 - me) * half, 128), half), :] = w_there[...]
    block = all_here.shape[0]
    rows_all = all_ref.shape[0]
    place(all_ref, me, (all_here, all_there), 0)
    at = lax.broadcasted_iota(jnp.int32, (batch, rows_all), 1)
    row = lax.broadcasted_iota(jnp.int32, (batch, rows_all), 0)
    base = (row // count % 2) * block + (row // count // 2) * 16
    pooled = dot_nn((at == base + row % count).astype(bf16), all_ref[...]).astype(bf16)
    pooled_ref[...] = pooled
    upper = dot_nn((at == base + count).astype(bf16), all_ref[:, :128])
    lower = dot_nn((at == base + count + 1).astype(bf16), all_ref[:, :128])
    lane = lax.broadcasted_iota(jnp.int32, (batch, 128), 1)
    line = lax.broadcasted_iota(jnp.int32, (batch, 128), 0)
    partner = jnp.sum(jnp.where(lane == line % count, upper * 64.0 + lower, 0.0), axis=1, keepdims=True)
    squash_float = jnp.tanh(dot_nn(pooled, w_ref[...]) + bias_ref[...])
    squash = squash_float.astype(bf16).astype(f32)
    inv_norm = lax.rsqrt(jnp.sum(squash * squash, axis=-1, keepdims=True) + 1e-06)
    unit = squash * inv_norm
    temp = jnp.exp(-temp_ref[0:1, 0:1])
    logits = dot_nt(unit, unit, precision=highest) * temp
    ids = lax.broadcasted_iota(jnp.int32, (batch, batch), 1)
    masked = jnp.where(ids == lax.broadcasted_iota(jnp.int32, (batch, batch), 0), -1e30, logits)
    row_top = jnp.max(masked, axis=-1, keepdims=True)
    row_expo = jnp.exp(masked - row_top)
    row_total = jnp.sum(row_expo, axis=-1, keepdims=True)
    chosen = (ids.astype(f32) == partner).astype(f32)
    row_loss = row_top + jnp.log(row_total) - jnp.sum(chosen * logits, axis=-1, keepdims=True)
    loss = jnp.sum(row_loss, axis=0, keepdims=True) / batch
    grad_logits = row_expo / row_total - chosen
    grad_temp = -jnp.sum(jnp.sum(grad_logits * logits, axis=-1, keepdims=True), axis=0, keepdims=True)
    grad_unit = jnp.dot(
        grad_logits + grad_logits.T, unit, precision=highest, preferred_element_type=f32
    ) * temp
    grad_squash = inv_norm * (grad_unit - unit * jnp.sum(unit * grad_unit, axis=-1, keepdims=True))
    grad_pre = (grad_squash * (1.0 - squash_float * squash_float)).astype(bf16)
    gw_ref[...] = dot_tn(pooled_ref[:, lanes_of(me, half)], grad_pre)
    gb_ref[...] = jnp.sum(grad_pre.astype(f32), axis=0, keepdims=True)
    grad_ref[...] = grad_pre.astype(f32)
    own = grad_ref[pl.ds(pl.multiple_of(rank_ref[0] * count, 8), count), :].astype(bf16)
    gp_ref[...] = dot_nt(own, w_ref[...])
    spot = lax.broadcasted_iota(jnp.int32, (8, 128), 1)
    scalars_ref[...] = jnp.where(spot == 0, loss, grad_temp)


def contrast_call(rank, me, gathered, w_here, w_there, bias, log_temp, count):
    width = w_here.shape[1]
    rows_all = 2 * gathered[0].shape[0]
    batch = rows_all // 16 * count
    half = w_here.shape[0]
    temp = jnp.broadcast_to(log_temp.reshape(1, 1), (8, 128))
    return call(
        functools.partial(contrast_kernel, count), "contrast", (1,), [rank, me],
        [(a, None, None) for a in (*gathered, w_here, w_there, bias.reshape(1, width), temp)],
        [
            ((half, width), f32, None, None),
            ((1, width), f32, None, None),
            ((count, width), f32, None, None),
            ((8, 128), f32, None, None),
        ],
        [
            pltpu.VMEM((rows_all, width), bf16),
            pltpu.VMEM((width, width), bf16),
            pltpu.VMEM((batch, width), bf16),
            pltpu.VMEM((batch, width), f32),
        ],
    )


def per_device(
    dp_size,
    tokens,
    qkv_weight,
    qv_bias,
    out_weight,
    out_bias,
    first_gain,
    first_shift,
    up_weight,
    up_bias,
    down_weight,
    down_bias,
    second_gain,
    second_shift,
    pool_weight,
    pool_bias,
    log_temp,
    segments,
    cls_pos,
    pair_index,
    attn_keep,
    ffn_keep,
    grad_out,
):
    me = lax.axis_index("tensor")
    here = lax.axis_index("dp")
    length = segments.shape[1]
    half = tokens.shape[1]
    units = up_bias.shape[0]
    me_one = me.reshape(1).astype(jnp.int32)
    ORDER.clear()
    here_one = here.reshape(1).astype(jnp.int32)
    spot = here_one & 3

    def ordered(mine, theirs, axis):
        return jnp.where(
            me == 0,
            jnp.concatenate([mine, theirs], axis),
            jnp.concatenate([theirs, mine], axis),
        )

    x_there = other(their_rows(me_one, [tokens], length)[0])
    qkv_there = other(qkv_weight)
    vec = jnp.concatenate(
        [qv_bias.reshape(-1), up_bias, out_bias, first_gain, first_shift, down_bias, second_gain, second_shift]
    ).reshape(1, -1)
    out_there = other(out_weight)
    up_there = other(up_weight)
    down_there = other(down_weight)
    pool_there = other(pool_weight)

    seg = lax.dynamic_slice_in_dim(segments, me, 1, 0)
    col = jnp.broadcast_to(seg.reshape(length, 1), (length, 128))
    cls = lax.dynamic_slice_in_dim(cls_pos, me, 1, 0).reshape(-1)
    qv_full, up_b, feats = vectors(me_one, vec, other(vec), units, half)

    x, q, k, v = project(me_one, tokens, x_there, qkv_weight, qkv_there, qv_full, length)
    sends = their_rows(me_one, [attn_keep, ffn_keep], length)
    keep1 = (attn_keep, other(sends[0]))
    keep2 = (ffn_keep, other(sends[1]))
    ctx, lse = attend(seg, col, q, k, v, [])
    res, low, act, slope, mixed, lay_mine, lay_theirs, pooled = feed_forward(
        me_one, cls, pair_index, ctx, x, out_weight, out_there, keep1, up_weight, up_there, down_weight, down_there,
        up_b, feats, keep2,
    )
    quick = dp_size == 16
    if quick:
        near = [pooled] + [across(pooled, m, dp_size) for m in (1, 2, 3)]
    go_there = other(their_rows(me_one, [grad_out], length)[0])
    if quick:
        (near,) = stage(here_one, ("join", near, 0))
        (all_here,) = stage(here_one, ("join", [near] + [across(near, m, dp_size) for m in (4, 8, 12)], 2))
        all_there = other(all_here)
    pool_rows = cls.shape[0]
    rank = here * 2 + me
    batch = dp_size * 2 * pool_rows
    if quick:
        grad_pool_w, grad_pool_b, grad_pooled, scalars = contrast_call(
            rank.reshape(1), me_one, [all_here, all_there], pool_weight, pool_there,
            pool_bias, log_temp, pool_rows,
        )
        grad_pool_b = grad_pool_b.reshape(-1)
        loss, grad_temp = scalars[0, 0], scalars[0, 1]
    else:
        gathered = lax.all_gather(pooled, ("dp", "tensor"), axis=0, tiled=True)
        pool_w = ordered(pool_weight, pool_there, 0)
        gathered = gathered.reshape(-1, pooled.shape[0], D)
        pooled_all = gathered[:, :pool_rows].reshape(-1, D)
        numbers = gathered[:, pool_rows : pool_rows + 2, :pool_rows].astype(jnp.int32)
        pairs_all = (numbers[:, 0] * 64 + numbers[:, 1]).reshape(-1)
        loss_total, grad_temp, grad_pool_pre = contrast(pooled_all, pool_w, pool_bias, log_temp, pairs_all)
        loss = loss_total / batch
        pooled_half = lax.dynamic_slice_in_dim(pooled_all, me * half, half, 1)
        grad_pool_w = dot_tn(pooled_half, grad_pool_pre)
        grad_pool_b = jnp.sum(grad_pool_pre, axis=0, dtype=f32)
        grad_pooled = dot_nt(lax.dynamic_slice_in_dim(grad_pool_pre, rank * pool_rows, pool_rows, 0), pool_w)

    layer_out = both_rows(me_one, lay_mine, other(lay_theirs))
    g, gm, sums2, gd_there = down_back(
        me_one, cls, mixed, grad_out, go_there, grad_pooled, feats, keep2, act
    )
    bit0, bit1 = here_one & 1, (here_one >> 1) & 1
    part, bias_there, gu_there = up_back(bit1, low, g, slope, up_there, down_there, False)
    down = down_own(bit0, act, g, other(gd_there))
    if quick:
        down = Chain(down, (0, 2, 3, 1), dp_size)
    part, bias_here, *up = up_back(bit1, low, g, slope, up_weight, down_weight, True, part, other(gu_there))
    if quick:
        up = Chain(up, (1, 0, 2, 3), dp_size)
    gr, grad_ctx, delta, sums1, go_there, go_here = out_back(
        me_one, gm, part, res, ctx, keep1, out_weight, out_there, feats, []
    )
    go_got = other(go_there)
    if quick:
        advance(here_one, down)
    grads = attend_back(seg, col, q, k, v, grad_ctx, lse, delta, tuple(range(D // PAIR)), [])
    if quick:
        advance(here_one, down, up)
    gq_there, gq_here = qkv_last(me_one, x, grads, bias_here, bias_there, sums1, sums2)
    rows = gq_here.shape[0] + D
    cuts = ((rows // 256 * 128, 0), (rows, 1))
    last = last_halves(here_one, gq_here, other(gq_there), go_here, go_got, cuts)
    if quick:
        orders = ((0, 1, 2, 3), (1, 0, 2, 3))
        last = [Chain(halves, order, dp_size) for halves, order in zip(last, orders)]
    gt_mine, gt_theirs = tokens_back(me_one, gr, grads, qkv_weight, qkv_there)
    if quick:
        while any(chain.step < 7 for chain in (down, up, *last)):
            for chain in (*last, down, up):
                if chain.step < 7:
                    advance(here_one, chain, free=True)
        down, up = down.parts, up.parts
        last = [chain.parts for chain in last]
    else:
        down, up = plain_sum(bit0[0], down), plain_sum(bit1[0], up)
        last = [plain_sum((here >> bit) & 1, halves) for halves, (_, bit) in zip(last, cuts)]
    grad_tokens = both_rows(me_one, gt_mine, other(gt_theirs))
    g_down_w = end(bit0, down, "down_end")
    g_up_w = end(bit1, up, "up_end")
    g_qkv_w, vec_sum, g_out_w = last_end(here_one, last, (0, 1), half)
    n_up = units // half
    return (
        layer_out,
        loss.reshape(1),
        grad_tokens,
        g_qkv_w,
        vec_sum[:2],
        g_out_w,
        vec_sum[2 + n_up],
        vec_sum[3 + n_up],
        vec_sum[4 + n_up],
        g_up_w,
        vec_sum[2 : 2 + n_up].reshape(-1),
        g_down_w,
        vec_sum[5 + n_up],
        vec_sum[6 + n_up],
        vec_sum[7 + n_up],
        grad_pool_w,
        grad_pool_b,
        grad_temp.reshape(1),
    )


def solution(mesh):
    return jax.shard_map(
        functools.partial(per_device, mesh.shape["dp"]),
        mesh=mesh,
        in_specs=(
            P("dp", "tensor"),
            P(None, None, "tensor"),
            P(None, "tensor"),
            P("tensor", None),
            P("tensor"),
            P("tensor"),
            P("tensor"),
            P(None, "tensor"),
            P("tensor"),
            P("tensor", None),
            P("tensor"),
            P("tensor"),
            P("tensor"),
            P("tensor", None),
            P(),
            P(),
            P("dp", None),
            P("dp", None),
            P("dp"),
            P("dp", "tensor"),
            P("dp", "tensor"),
            P("dp", "tensor"),
        ),
        out_specs=(
            P("dp", "tensor"),
            P(),
            P("dp", "tensor"),
            P(None, None, "tensor"),
            P(None, "tensor"),
            P("tensor", None),
            P("tensor"),
            P("tensor"),
            P("tensor"),
            P(None, "tensor"),
            P("tensor"),
            P("tensor", None),
            P("tensor"),
            P("tensor"),
            P("tensor"),
            P("tensor", None),
            P(),
            P(),
        ),
        check_vma=False,
    )
```

profile of v0, /device:TPU:0, one launch (start us, length us, event | category | flops | bytes accessed | tf_op | source)
XLA Modules:
  0.0 333.7 jit_solution(6033958039170470002)
XLA Ops:
  1.3 2.1 their_rows.3.refs_3_
  6.4 7.2 %qkv.1 = (bf16[1024,768]{1,0:T(8,128)(2,1)S(1)}, bf16[1024,768]{1,0:T(8,128)(2,1)S(1)}, bf16[1024,768]{1,0:T(8,128)(2,1)S(1)}, bf16[1024,768]{1,0:T(8,128)(2,1)S(1)}) custom-call(s32[1]{0:T(128)} %bitcast.refs_0_.refs_1_, bf16[2048,384]{1,0:T(8,128)(2,1)} %refs_1_.5, bf16[1024,384]{1,0:T(8,128)(2,1)} %collective-permute-done.refs_2_, ...), custom_call_target="tpu_custom_call" | custom-call | flops 5750000128 | bytes 1000 | tf_op jit(solution)/shard_map/qkv/pallas_call | solution.py:83
  13.6 4.1 %their_rows.4 = (bf16[1024,384]{1,0:T(8,128)(2,1)S(1)}, bf16[1024,384]{1,0:T(8,128)(2,1)S(1)}) custom-call(s32[1]{0:T(128)} %bitcast.refs_0_.refs_1_, s32[2048,384]{1,0:T(8,128)} %refs_5_.6, s32[2048,384]{1,0:T(8,128)} %refs_7_.4, bf16[1024,768]{1,0:T(8,128)(2,1)S(1)} %get-tuple-element.102.refs_3_.refs_4_.refs_1_), custom_call_target="tpu_custom_call" | custom-call | flops 2300000000 | bytes 1000 | tf_op jit(solution)/shard_map/their_rows/pallas_call | solution.py:83
  18.6 13.5 %attend.1 = (bf16[1024,768]{1,0:T(8,128)(2,1)S(1)}, f32[16,1024]{1,0:T(8,128)S(1)}) custom-call(s32[1024]{0:T(1024)} %bitcast.11, s32[1024,128]{1,0:T(8,128)S(1)} %broadcast_in_dim.12.refs_1_, s32[1,1024]{1,0:T(1,128)} %copy-done.35, bf16[1024,768]{1,0:T(8,128)(2,1)} %copy-done.19, bf16[1024,768]{1,0:T(8,128)(2,1)S(1)} %get-tuple-element.100.refs_4_, ...), custom_call_target="tpu_custom_call" | custom-call | flops 12650000384 | bytes 1000 | tf_op jit(solution)/shard_map/attend/pallas_call | solution.py:83
  32.1 26.3 %ffn.1 = (f32[1024,768]{1,0:T(8,128)S(1)}, bf16[1024,768]{1,0:T(8,128)(2,1)S(1)}, bf16[1024,3072]{1,0:T(8,128)(2,1)}, bf16[1024,3072]{1,0:T(8,128)(2,1)}, f32[10...) custom-call(s32[1]{0:T(128)} %bitcast.refs_0_.refs_1_, ...), custom_call_target="tpu_custom_call" | custom-call | flops 28750000128 | bytes 1000 | tf_op jit(solution)/shard_map/ffn/pallas_call | solution.py:83
  59.6 2.1 collective-permute-start.9
  64.0 2.2 their_rows.5.refs_5_
  67.6 3.0 collective-permute-start.12
  70.6 1.7 collective-permute-start.13
  73.7 7.2 %collective-permute-done.13.refs_3_ = bf16[64,768]{1,0:T(8,128)(2,1)S(1)} collective-permute-done((bf16[64,768]{1,0:T(8,128)(2,1)S(1)}, bf16[64,768]{1,0:T(8,128)(2,1)S(1)}, u32[]{:S(2)}, u32[]{:S(2)}) %collective-permute-start.13) | collective-permute-done | bytes 98336 | tf_op jit(solution)/shard_map/ppermute | solution.py:774
  83.0 1.4 collective-permute-done.15.refs_3_
  84.4 7.1 %contrast.1 = (f32[384,768]{1,0:T(8,128)}, f32[1,768]{1,0:T(1,128)S(1)}, f32[8,768]{1,0:T(8,128)S(1)}, f32[8,128]{1,0:T(8,128)S(1)}) custom-call(s32[1]{0:T(128)} %bitcast.3.refs_0_, s32[1]{0:T(128)} %bitcast.refs_0_.refs_1_, bf16[256,768]{1,0:T(8,128)(2,1)} %stage.30.refs_2_.refs_8_, bf16[256,768]{1,0:T(8,128)(2,1)} %collective-permute-done.15.refs_3_, ...), custom_call_target="tpu_custom_call" | custom-call | flops 6899999744 | bytes 1000 | tf_op jit(solution)/shard_map/contrast/pallas_call | solution.py:83
  91.6 9.0 %down_back.1 = (bf16[1024,768]{1,0:T(8,128)(2,1)S(1)}, f32[1024,768]{1,0:T(8,128)S(1)}, f32[8,768]{1,0:T(8,128)S(1)}, bf16[1536,768]{1,0:T(8,128)(2,1)S(1)}) custom-call(s32[1]{0:T(128)} %bitcast.refs_0_.refs_1_, s32[8]{0:T(128)S(1)} %dynamic-slice_bitcast_fusion.refs_1_, f32[1024,768]{1,0:T(8,128)S(1)} %copy-done.27, bf16[2048,384]{1,0:T(8,128)(2,1)} %refs_3_.3, ...), custom_call_target="tpu_custom_call" | custom-call | flops 10350000128 | bytes 1000 | tf_op jit(solution)/shard_map/down_back/pallas_call | solution.py:83
  100.8 10.6 %up_back.1 = (f32[1024,768]{1,0:T(8,128)S(1)}, f32[1,1536]{1,0:T(1,128)S(1)}, bf16[768,1536]{1,0:T(8,128)(2,1)S(1)}) custom-call(s32[1]{0:T(128)S(6)} %and.8.refs_0_, bf16[1024,768]{1,0:T(8,128)(2,1)S(1)} %copy-done.29, bf16[1024,768]{1,0:T(8,128)(2,1)S(1)} %get-tuple-element.119.refs_2_, bf16[1024,3072]{1,0:T(8,128)(2,1)} %get-tuple-element.120.refs_3_, ...), custom_call_target="tpu_custom_call" | custom-call | flops 11500000256 | bytes 1000 | tf_op jit(solution)/shard_map/up_back/pallas_call | solution.py:83
  111.8 1.4 copy-done.46
  113.2 5.1 %down_own.1 = (bf16[768,768]{1,0:T(8,128)(2,1)S(1)}, bf16[768,768]{1,0:T(8,128)(2,1)S(1)}) custom-call(s32[1]{0:T(128)S(6)} %and.9.refs_0_, bf16[1024,3072]{1,0:T(8,128)(2,1)} %get-tuple-element.115.refs_9_.refs_1_, bf16[1024,768]{1,0:T(8,128)(2,1)S(1)} %get-tuple-element.119.refs_2_, bf16[1536,768]{1,0:T(8,128)(2,1)} %copy-done.46, ...), custom_call_target="tpu_custom_call" | custom-call | flops 4024999936 | bytes 1000 | tf_op jit(solution)/shard_map/down_own/pallas_call | solution.py:83
  119.9 11.1 %up_own.1 = (f32[1024,768]{1,0:T(8,128)S(1)}, f32[1,1536]{1,0:T(1,128)S(1)}, bf16[384,1536]{1,0:T(8,128)(2,1)S(1)}, bf16[384,1536]{1,0:T(8,128)(2,1)S(1)}) custom-call(s32[1]{0:T(128)S(6)} %and.8.refs_0_, bf16[1024,768]{1,0:T(8,128)(2,1)S(1)} %copy-done.29, bf16[1024,768]{1,0:T(8,128)(2,1)S(1)} %get-tuple-element.119.refs_2_, ...), custom_call_target="tpu_custom_call" | custom-call | flops 11500000256 | bytes 1000 | tf_op jit(solution)/shard_map/up_own/pallas_call | solution.py:83
  132.1 9.0 %out_back.1 = (f32[1024,768]{1,0:T(8,128)S(1)}, bf16[1024,768]{1,0:T(8,128)(2,1)S(1)}, f32[16,1024]{1,0:T(8,128)S(1)}, f32[8,768]{1,0:T(8,128)S(1)}, bf16[384,76...) custom-call(s32[1]{0:T(128)} %bitcast.refs_0_.refs_1_, f32[1024,768]{1,0:T(8,128)S(1)} %get-tuple-element.117.refs_1_, ...), custom_call_target="tpu_custom_call" | custom-call | flops 10350000128 | bytes 1000 | tf_op jit(solution)/shard_map/out_back/pallas_call | solution.py:83
  142.3 4.1 %collective-permute-done.20.refs_2_ = bf16[768,768]{1,0:T(8,128)(2,1)S(1)} collective-permute-done((bf16[768,768]{1,0:T(8,128)(2,1)S(1)}, bf16[768,768]{1,0:T(8,128)(2,1)S(1)}, u32[]{:S(2)}, u32[]{:S(2)}) %collective-permute-start.20) | collective-permute-done | bytes 1179680 | tf_op jit(solution)/shard_map/ppermute | solution.py:774
  147.0 2.0 collective-permute-start.21
  148.9 20.1 %attend_back.1 = (bf16[1024,768]{1,0:T(8,128)(2,1)S(1)}, bf16[1024,768]{1,0:T(8,128)(2,1)S(1)}, bf16[1024,768]{1,0:T(8,128)(2,1)S(1)}) custom-call(s32[1024]{0:T(1024)} %bitcast.12, s32[1024,128]{1,0:T(8,128)S(1)} %broadcast_in_dim.12.refs_1_, s32[1,1024]{1,0:T(1,128)} %copy-done.35, bf16[1024,768]{1,0:T(8,128)(2,1)} %copy-done.19, ...), custom_call_target="tpu_custom_call" | custom-call | flops 24149999616 | bytes 1000 | tf_op jit(solution)/shard_map/attend_back/pallas_call | solution.py:83
  171.1 4.1 %qkv_last.1 = (bf16[2432,384]{1,0:T(8,128)(2,1)S(1)}, bf16[2432,384]{1,0:T(8,128)(2,1)S(1)}) custom-call(s32[1]{0:T(128)} %bitcast.refs_0_.refs_1_, bf16[1024,768]{1,0:T(8,128)(2,1)S(1)} %copy-done.15, bf16[1024,768]{1,0:T(8,128)(2,1)S(1)} %get-tuple-element.136.refs_5_.refs_2_, bf16[1024,768]{1,0:T(8,128)(2,1)S(1)} %get-tuple-element.137.refs_3_, ...), custom_call_target="tpu_custom_call" | custom-call | flops 4600000000 | bytes 1000 | tf_op jit(solution)/shard_map/qkv_last/pallas_call | solution.py:83
  175.2 1.6 collective-permute-start.49
  177.0 14.9 %collective-permute-done.49.refs_2_ = bf16[192,768]{1,0:T(8,128)(2,1)S(1)} collective-permute-done((bf16[192,768]{1,0:T(8,128)(2,1)S(1)}, bf16[192,768]{1,0:T(8,128)(2,1)S(1)}, u32[]{:S(2)}, u32[]{:S(2)}) %collective-permute-start.49) | collective-permute-done | bytes 294944 | tf_op jit(solution)/shard_map/ppermute | solution.py:774
  192.1 5.4 %collective-permute-done.50.refs_2_ = bf16[96,768]{1,0:T(8,128)(2,1)S(1)} collective-permute-done((bf16[96,768]{1,0:T(8,128)(2,1)S(1)}, bf16[96,768]{1,0:T(8,128)(2,1)S(1)}, u32[]{:S(2)}, u32[]{:S(2)}) %collective-permute-start.50) | collective-permute-done | bytes 147488 | tf_op jit(solution)/shard_map/ppermute | solution.py:774
  198.4 4.3 %collective-permute-done.51.refs_2_ = bf16[96,768]{1,0:T(8,128)(2,1)S(1)} collective-permute-done((bf16[96,768]{1,0:T(8,128)(2,1)S(1)}, bf16[96,768]{1,0:T(8,128)(2,1)S(1)}, u32[]{:S(2)}, u32[]{:S(2)}) %collective-permute-start.51) | collective-permute-done | bytes 147488 | tf_op jit(solution)/shard_map/ppermute | solution.py:774
  204.0 4.2 %collective-permute-done.43.refs_2_ = bf16[96,1536]{1,0:T(8,128)(2,1)S(1)} collective-permute-done((bf16[96,1536]{1,0:T(8,128)(2,1)S(1)}, bf16[96,1536]{1,0:T(8,128)(2,1)S(1)}, u32[]{:S(2)}, u32[]{:S(2)}) %collective-permute-start.43) | collective-permute-done | bytes 294944 | tf_op jit(solution)/shard_map/ppermute | solution.py:774
  208.6 2.0 collective-permute-start.34
  210.6 12.3 %collective-permute-done.44.refs_2_ = bf16[48,1536]{1,0:T(8,128)(2,1)S(1)} collective-permute-done((bf16[48,1536]{1,0:T(8,128)(2,1)S(1)}, bf16[48,1536]{1,0:T(8,128)(2,1)S(1)}, u32[]{:S(2)}, u32[]{:S(2)}) %collective-permute-start.44) | collective-permute-done | bytes 147488 | tf_op jit(solution)/shard_map/ppermute | solution.py:774
  223.2 2.3 collective-permute-start.53
  225.6 4.6 %collective-permute-done.45.refs_2_ = bf16[48,1536]{1,0:T(8,128)(2,1)S(1)} collective-permute-done((bf16[48,1536]{1,0:T(8,128)(2,1)S(1)}, bf16[48,1536]{1,0:T(8,128)(2,1)S(1)}, u32[]{:S(2)}, u32[]{:S(2)}) %collective-permute-start.45) | collective-permute-done | bytes 147488 | tf_op jit(solution)/shard_map/ppermute | solution.py:774
  231.9 14.5 %collective-permute-done.46.refs_2_ = bf16[96,1536]{1,0:T(8,128)(2,1)S(1)} collective-permute-done((bf16[96,1536]{1,0:T(8,128)(2,1)S(1)}, bf16[96,1536]{1,0:T(8,128)(2,1)S(1)}, u32[]{:S(2)}, u32[]{:S(2)}) %collective-permute-start.46) | collective-permute-done | bytes 294944 | tf_op jit(solution)/shard_map/ppermute | solution.py:774
  247.3 1.9 collective-permute-start.54
  249.3 2.0 collective-permute-start.36
  251.4 2.8 collective-permute-done.28.refs_2_
  256.2 7.2 %tokens_back.1 = (f32[1024,384]{1,0:T(8,128)S(1)}, f32[1024,384]{1,0:T(8,128)S(1)}) custom-call(s32[1]{0:T(128)} %bitcast.refs_0_.refs_1_, f32[1024,768]{1,0:T(8,128)} %copy-done.17, bf16[1024,768]{1,0:T(8,128)(2,1)} %copy-done.2, bf16[1024,768]{1,0:T(8,128)(2,1)S(1)} %get-tuple-element.137.refs_3_, bf16[1024,768]{1,0:T(8,128)(2,1)S(1)} %get-tuple-element.138.refs_4_, ...), custom_call_target="tpu_custom_call" | custom-call | flops 5750000128 | bytes 1000 | tf_op jit(solution)/shard_map/tokens_back/pallas_call | solution.py:83
  265.7 5.1 %collective-permute-done.30.refs_2_ = bf16[96,384]{1,0:T(8,128)(2,1)S(1)} collective-permute-done((bf16[96,384]{1,0:T(8,128)(2,1)S(1)}, bf16[96,384]{1,0:T(8,128)(2,1)S(1)}, u32[]{:S(2)}, u32[]{:S(2)}) %collective-permute-start.30) | collective-permute-done | bytes 73760 | tf_op jit(solution)/shard_map/ppermute | solution.py:774
  271.0 5.4 %collective-permute-done.37.refs_2_ = bf16[104,384]{1,0:T(8,128)(2,1)S(1)} collective-permute-done((bf16[104,384]{1,0:T(8,128)(2,1)S(1)}, bf16[104,384]{1,0:T(8,128)(2,1)S(1)}, u32[]{:S(2)}, u32[]{:S(2)}) %collective-permute-start.37) | collective-permute-done | bytes 79904 | tf_op jit(solution)/shard_map/ppermute | solution.py:774
  276.5 2.5 collective-permute-start.38
  280.3 2.3 collective-permute-done.38.refs_2_
  283.5 1.4 collective-permute-start.39
  286.2 2.7 collective-permute-done.39.refs_2_
  290.2 3.9 %both_rows.2 = bf16[2048,384]{1,0:T(8,128)(2,1)} custom-call(s32[1]{0:T(128)} %bitcast.refs_0_.refs_1_, bf16[1024,384]{1,0:T(8,128)(2,1)} %copy-done.18, bf16[1024,384]{1,0:T(8,128)(2,1)} %collective-permute-done.8.refs_2_), custom_call_target="tpu_custom_call" | custom-call | flops 2300000000 | bytes 1000 | tf_op jit(solution)/shard_map/both_rows/pallas_call | solution.py:83
  294.1 20.6 %collective-permute-done.32.refs_2_ = bf16[384,384]{1,0:T(8,128)(2,1)S(1)} collective-permute-done((bf16[384,384]{1,0:T(8,128)(2,1)S(1)}, bf16[384,384]{1,0:T(8,128)(2,1)S(1)}, u32[]{:S(2)}, u32[]{:S(2)}) %collective-permute-start.32) | collective-permute-done | bytes 294944 | tf_op jit(solution)/shard_map/ppermute | solution.py:774
  316.0 3.8 %down_end.1 = f32[1536,768]{1,0:T(8,128)} custom-call(s32[1]{0:T(128)S(6)} %and.9.refs_0_, bf16[768,768]{1,0:T(8,128)(2,1)S(1)} %stage.57.refs_1_, bf16[768,768]{1,0:T(8,128)(2,1)} %collective-permute-done.54.refs_2_), custom_call_target="tpu_custom_call" | custom-call | flops 3449999872 | bytes 1000 | tf_op jit(solution)/shard_map/down_end/pallas_call | solution.py:83
  319.9 4.2 %up_end.1 = f32[768,1536]{1,0:T(8,128)} custom-call(s32[1]{0:T(128)S(6)} %and.8.refs_0_, bf16[384,1536]{1,0:T(8,128)(2,1)} %stage.52.refs_1_, bf16[384,1536]{1,0:T(8,128)(2,1)} %collective-permute-done.48.refs_2_), custom_call_target="tpu_custom_call" | custom-call | flops 3449999872 | bytes 1000 | tf_op jit(solution)/shard_map/up_end/pallas_call | solution.py:83
  324.1 4.9 %both_rows.3 = f32[2048,384]{1,0:T(8,128)} custom-call(s32[1]{0:T(128)} %bitcast.refs_0_.refs_1_, f32[1024,384]{1,0:T(8,128)} %copy-done.16, f32[1024,384]{1,0:T(8,128)} %collective-permute-done.25.refs_2_), custom_call_target="tpu_custom_call" | custom-call | flops 2300000000 | bytes 1000 | tf_op jit(solution)/shard_map/both_rows/pallas_call | solution.py:83
  329.0 2.7 last_end.1
  (231 shorter events, 37.2 us)
Async XLA Ops:
  0.7 5.6 %collective-permute-start.1 = (bf16[3,768,384]{2,1,0:T(8,128)(2,1)}, bf16[3,768,384]{2,1,0:T(8,128)(2,1)S(1)}, u32[]{:S(2)}, u32[]{:S(2)}) collective-permute-start(bf16[3,768,384]{2,1,0:T(8,128)(2,1)} %refs_5_.7), channel_id=1, source_target_pairs={{0,1},{1,0},{2,3},{3,2},{4,5},{5,4},{6,7},{7,6},{8,9},{9,8},{10,11... | collective-permute-start | bytes 5308424 | tf_op jit(solution)/shard_map/ppermute | solution.py:770
  3.5 28.5 %collective-permute-start.5 = (bf16[768,1536]{1,0:T(8,128)(2,1)}, bf16[768,1536]{1,0:T(8,128)(2,1)}, u32[]{:S(2)}, u32[]{:S(2)}) collective-permute-start(bf16[768,1536]{1,0:T(8,128)(2,1)} %refs_4_.3), channel_id=1, source_target_pairs={{0,1},{1,0},{2,3},{3,2},{4,5},{5,4},{6,7},{7,6},{8,9},{9,8},{10,11... | collective-permute-start | bytes 7077896 | tf_op jit(solution)/shard_map/ppermute | solution.py:770
  4.0 28.1 %collective-permute-start.6 = (bf16[1536,768]{1,0:T(8,128)(2,1)}, bf16[1536,768]{1,0:T(8,128)(2,1)}, u32[]{:S(2)}, u32[]{:S(2)}) collective-permute-start(bf16[1536,768]{1,0:T(8,128)(2,1)} %refs_5_.5), channel_id=1, source_target_pairs={{0,1},{1,0},{2,3},{3,2},{4,5},{5,4},{6,7},{7,6},{8,9},{9,8},{10,11... | collective-permute-start | bytes 7077896 | tf_op jit(solution)/shard_map/ppermute | solution.py:770
  6.1 25.9 %collective-permute-start.3 = (bf16[384,768]{1,0:T(8,128)(2,1)S(1)}, bf16[384,768]{1,0:T(8,128)(2,1)S(1)}, u32[]{:S(2)}, u32[]{:S(2)}) collective-permute-start(bf16[384,768]{1,0:T(8,128)(2,1)S(1)} %copy-done.9), channel_id=1, source_target_pairs={{0,1},{1,0},{2,3},{3,2},{4,5},{5,4},{6,7},{7,6},{8,9},{9,8},{10,11... | collective-permute-start | bytes 1769480 | tf_op jit(solution)/shard_map/ppermute | solution.py:770
  17.8 14.3 %collective-permute-start.4 = (bf16[1024,384]{1,0:T(8,128)(2,1)S(1)}, bf16[1024,384]{1,0:T(8,128)(2,1)S(1)}, u32[]{:S(2)}, u32[]{:S(2)}) collective-permute-start(bf16[1024,384]{1,0:T(8,128)(2,1)S(1)} %get-tuple-element.103.refs_6_), channel_id=1, source_target_pairs={{0,1},{1,0},{2,3},{3,2},{4,5},{5,4},{6,7},{7,6},{8,9},{9,8},{10,11... | collective-permute-start | bytes 2359304 | tf_op jit(solution)/shard_map/ppermute | solution.py:770
  18.2 13.9 %collective-permute-start.7 = (bf16[1024,384]{1,0:T(8,128)(2,1)S(1)}, bf16[1024,384]{1,0:T(8,128)(2,1)S(1)}, u32[]{:S(2)}, u32[]{:S(2)}) collective-permute-start(bf16[1024,384]{1,0:T(8,128)(2,1)S(1)} %get-tuple-element.107), channel_id=1, source_target_pairs={{0,1},{1,0},{2,3},{3,2},{4,5},{5,4},{6,7},{7,6},{8,9},{9,8},{10,11... | collective-permute-start | bytes 2359304 | tf_op jit(solution)/shard_map/ppermute | solution.py:770
  59.6 6.6 %collective-permute-start.9 = (bf16[16,768]{1,0:T(8,128)(2,1)S(1)}, bf16[16,768]{1,0:T(8,128)(2,1)S(1)}, u32[]{:S(2)}, u32[]{:S(2)}) collective-permute-start(bf16[16,768]{1,0:T(8,128)(2,1)S(1)} %get-tuple-element.111.refs_2_.refs_1_), channel_id=1, source_target_pairs={{0,2},{2,0},{4,6},{6,4},{8,10},{10,8},{12,14},{14,12},{16,18},{18,... | collective-permute-start | bytes 73736 | tf_op jit(solution)/shard_map/ppermute | solution.py:774
  67.6 6.2 %collective-permute-start.12 = (bf16[64,768]{1,0:T(8,128)(2,1)S(1)}, bf16[64,768]{1,0:T(8,128)(2,1)S(1)}, u32[]{:S(2)}, u32[]{:S(2)}) collective-permute-start(bf16[64,768]{1,0:T(8,128)(2,1)S(1)} %stage.29.refs_1_.refs_5_), channel_id=1, source_target_pairs={{0,8},{2,10},{4,12},{6,14},{8,0},{10,2},{12,4},{14,6},{16,24},{18,... | collective-permute-start | bytes 294920 | tf_op jit(solution)/shard_map/ppermute | solution.py:774
  70.6 10.4 %collective-permute-start.13 = (bf16[64,768]{1,0:T(8,128)(2,1)S(1)}, bf16[64,768]{1,0:T(8,128)(2,1)S(1)}, u32[]{:S(2)}, u32[]{:S(2)}) collective-permute-start(bf16[64,768]{1,0:T(8,128)(2,1)S(1)} %stage.29.refs_1_.refs_5_), channel_id=1, source_target_pairs={{0,16},{2,18},{4,20},{6,22},{8,24},{10,26},{12,28},{14,30},{16,0},... | collective-permute-start | bytes 294920 | tf_op jit(solution)/shard_map/ppermute | solution.py:774
  72.3 8.7 %collective-permute-start.14 = (bf16[64,768]{1,0:T(8,128)(2,1)S(1)}, bf16[64,768]{1,0:T(8,128)(2,1)S(1)}, u32[]{:S(2)}, u32[]{:S(2)}) collective-permute-start(bf16[64,768]{1,0:T(8,128)(2,1)S(1)} %stage.29.refs_1_.refs_5_), channel_id=1, source_target_pairs={{0,24},{2,26},{4,28},{6,30},{8,16},{10,18},{12,20},{14,22},{16,8},... | collective-permute-start | bytes 294920 | tf_op jit(solution)/shard_map/ppermute | solution.py:774
  73.0 10.0 %collective-permute-start.16 = (bf16[384,768]{1,0:T(8,128)(2,1)S(1)}, bf16[384,768]{1,0:T(8,128)(2,1)}, u32[]{:S(2)}, u32[]{:S(2)}) collective-permute-start(bf16[384,768]{1,0:T(8,128)(2,1)S(1)} %copy-done.8), channel_id=1, source_target_pairs={{0,1},{1,0},{2,3},{3,2},{4,5},{5,4},{6,7},{7,6},{8,9},{9,8},{10,11... | collective-permute-start | bytes 1769480 | tf_op jit(solution)/shard_map/ppermute | solution.py:770
  81.8 9.7 %collective-permute-start.17 = (bf16[1024,384]{1,0:T(8,128)(2,1)S(1)}, bf16[1024,384]{1,0:T(8,128)(2,1)S(1)}, u32[]{:S(2)}, u32[]{:S(2)}) collective-permute-start(bf16[1024,384]{1,0:T(8,128)(2,1)S(1)} %their_rows.5.refs_5_), channel_id=1, source_target_pairs={{0,1},{1,0},{2,3},{3,2},{4,5},{5,4},{6,7},{7,6},{8,9},{9,8},{10,11... | collective-permute-start | bytes 2359304 | tf_op jit(solution)/shard_map/ppermute | solution.py:770
  100.6 11.3 %collective-permute-start.19 = (bf16[1536,768]{1,0:T(8,128)(2,1)S(1)}, bf16[1536,768]{1,0:T(8,128)(2,1)S(1)}, u32[]{:S(2)}, u32[]{:S(2)}) collective-permute-start(bf16[1536,768]{1,0:T(8,128)(2,1)S(1)} %get-tuple-element.124), channel_id=1, source_target_pairs={{0,1},{1,0},{2,3},{3,2},{4,5},{5,4},{6,7},{7,6},{8,9},{9,8},{10,11... | collective-permute-start | bytes 7077896 | tf_op jit(solution)/shard_map/ppermute | solution.py:770
  111.4 7.1 %collective-permute-start.18 = (bf16[768,1536]{1,0:T(8,128)(2,1)S(1)}, bf16[768,1536]{1,0:T(8,128)(2,1)S(1)}, u32[]{:S(2)}, u32[]{:S(2)}) collective-permute-start(bf16[768,1536]{1,0:T(8,128)(2,1)S(1)} %get-tuple-element.123), channel_id=1, source_target_pairs={{0,1},{1,0},{2,3},{3,2},{4,5},{5,4},{6,7},{7,6},{8,9},{9,8},{10,11... | collective-permute-start | bytes 7077896 | tf_op jit(solution)/shard_map/ppermute | solution.py:770
  118.3 28.1 %collective-permute-start.20 = (bf16[768,768]{1,0:T(8,128)(2,1)S(1)}, bf16[768,768]{1,0:T(8,128)(2,1)S(1)}, u32[]{:S(2)}, u32[]{:S(2)}) collective-permute-start(bf16[768,768]{1,0:T(8,128)(2,1)S(1)} %get-tuple-element.133), channel_id=1, source_target_pairs={{0,2},{2,0},{4,6},{6,4},{8,10},{10,8},{12,14},{14,12},{16,18},{18,... | collective-permute-start | bytes 3538952 | tf_op jit(solution)/shard_map/ppermute | solution.py:774
  131.0 38.1 %collective-permute-start.22 = (bf16[384,1536]{1,0:T(8,128)(2,1)S(1)}, bf16[384,1536]{1,0:T(8,128)(2,1)S(1)}, u32[]{:S(2)}, u32[]{:S(2)}) collective-permute-start(bf16[384,1536]{1,0:T(8,128)(2,1)S(1)} %get-tuple-element.141), channel_id=1, source_target_pairs={{0,4},{2,6},{4,0},{6,2},{8,12},{10,14},{12,8},{14,10},{16,20},{18,... | collective-permute-start | bytes 3538952 | tf_op jit(solution)/shard_map/ppermute | solution.py:774
  147.0 22.1 %collective-permute-start.21 = (bf16[384,768]{1,0:T(8,128)(2,1)S(1)}, bf16[384,768]{1,0:T(8,128)(2,1)S(1)}, u32[]{:S(2)}, u32[]{:S(2)}) collective-permute-start(bf16[384,768]{1,0:T(8,128)(2,1)S(1)} %get-tuple-element.139), channel_id=1, source_target_pairs={{0,8},{2,10},{4,12},{6,14},{8,0},{10,2},{12,4},{14,6},{16,24},{18,... | collective-permute-start | bytes 1769480 | tf_op jit(solution)/shard_map/ppermute | solution.py:774
  175.2 27.7 %collective-permute-start.23 = (bf16[2432,384]{1,0:T(8,128)(2,1)S(1)}, bf16[2432,384]{1,0:T(8,128)(2,1)S(1)}, u32[]{:S(2)}, u32[]{:S(2)}) collective-permute-start(bf16[2432,384]{1,0:T(8,128)(2,1)S(1)} %get-tuple-element.144.refs_5_), channel_id=1, source_target_pairs={{0,1},{1,0},{2,3},{3,2},{4,5},{5,4},{6,7},{7,6},{8,9},{9,8},{10,11... | collective-permute-start | bytes 5603336 | tf_op jit(solution)/shard_map/ppermute | solution.py:770
  175.2 16.6 %collective-permute-start.49 = (bf16[192,768]{1,0:T(8,128)(2,1)S(1)}, bf16[192,768]{1,0:T(8,128)(2,1)S(1)}, u32[]{:S(2)}, u32[]{:S(2)}) collective-permute-start(bf16[192,768]{1,0:T(8,128)(2,1)S(1)} %get-tuple-element.174), channel_id=1, source_target_pairs={{0,16},{2,18},{4,20},{6,22},{8,24},{10,26},{12,28},{14,30},{16,0},... | collective-permute-start | bytes 884744 | tf_op jit(solution)/shard_map/ppermute | solution.py:774
  176.8 21.2 %collective-permute-start.42 = (bf16[192,1536]{1,0:T(8,128)(2,1)S(1)}, bf16[192,1536]{1,0:T(8,128)(2,1)S(1)}, u32[]{:S(2)}, u32[]{:S(2)}) collective-permute-start(bf16[192,1536]{1,0:T(8,128)(2,1)S(1)} %get-tuple-element.169), channel_id=1, source_target_pairs={{0,2},{2,0},{4,6},{6,4},{8,10},{10,8},{12,14},{14,12},{16,18},{18,... | collective-permute-start | bytes 1769480 | tf_op jit(solution)/shard_map/ppermute | solution.py:774
  176.8 26.0 %collective-permute-start.24 = (bf16[384,768]{1,0:T(8,128)(2,1)S(1)}, bf16[384,768]{1,0:T(8,128)(2,1)S(1)}, u32[]{:S(2)}, u32[]{:S(2)}) collective-permute-start(bf16[384,768]{1,0:T(8,128)(2,1)S(1)} %get-tuple-element.146), channel_id=1, source_target_pairs={{0,1},{1,0},{2,3},{3,2},{4,5},{5,4},{6,7},{7,6},{8,9},{9,8},{10,11... | collective-permute-start | bytes 1769480 | tf_op jit(solution)/shard_map/ppermute | solution.py:770
  192.0 5.5 %collective-permute-start.50 = (bf16[96,768]{1,0:T(8,128)(2,1)S(1)}, bf16[96,768]{1,0:T(8,128)(2,1)S(1)}, u32[]{:S(2)}, u32[]{:S(2)}) collective-permute-start(bf16[96,768]{1,0:T(8,128)(2,1)S(1)} %get-tuple-element.176), channel_id=1, source_target_pairs={{0,4},{2,6},{4,0},{6,2},{8,12},{10,14},{12,8},{14,10},{16,20},{18,... | collective-permute-start | bytes 442376 | tf_op jit(solution)/shard_map/ppermute | solution.py:774
  198.3 10.0 %collective-permute-start.43 = (bf16[96,1536]{1,0:T(8,128)(2,1)S(1)}, bf16[96,1536]{1,0:T(8,128)(2,1)S(1)}, u32[]{:S(2)}, u32[]{:S(2)}) collective-permute-start(bf16[96,1536]{1,0:T(8,128)(2,1)S(1)} %get-tuple-element.171), channel_id=1, source_target_pairs={{0,8},{2,10},{4,12},{6,14},{8,0},{10,2},{12,4},{14,6},{16,24},{18,... | collective-permute-start | bytes 884744 | tf_op jit(solution)/shard_map/ppermute | solution.py:774
  202.8 20.2 %collective-permute-start.52 = (bf16[192,768]{1,0:T(8,128)(2,1)S(1)}, bf16[192,768]{1,0:T(8,128)(2,1)S(1)}, u32[]{:S(2)}, u32[]{:S(2)}) collective-permute-start(bf16[192,768]{1,0:T(8,128)(2,1)S(1)} %stage.55.refs_1_), channel_id=1, source_target_pairs={{0,16},{2,18},{4,20},{6,22},{8,24},{10,26},{12,28},{14,30},{16,0},... | collective-permute-start | bytes 884744 | tf_op jit(solution)/shard_map/ppermute | solution.py:774
  204.0 26.3 %collective-permute-start.26 = (bf16[768,384]{1,0:T(8,128)(2,1)S(1)}, bf16[768,384]{1,0:T(8,128)(2,1)S(1)}, u32[]{:S(2)}, u32[]{:S(2)}) collective-permute-start(bf16[768,384]{1,0:T(8,128)(2,1)S(1)} %get-tuple-element.150), channel_id=1, source_target_pairs={{0,2},{2,0},{4,6},{6,4},{8,10},{10,8},{12,14},{14,12},{16,18},{18,... | collective-permute-start | bytes 1769480 | tf_op jit(solution)/shard_map/ppermute | solution.py:774
  208.4 14.5 %collective-permute-start.44 = (bf16[48,1536]{1,0:T(8,128)(2,1)S(1)}, bf16[48,1536]{1,0:T(8,128)(2,1)S(1)}, u32[]{:S(2)}, u32[]{:S(2)}) collective-permute-start(bf16[48,1536]{1,0:T(8,128)(2,1)S(1)} %get-tuple-element.173), channel_id=1, source_target_pairs={{0,16},{2,18},{4,20},{6,22},{8,24},{10,26},{12,28},{14,30},{16,0},... | collective-permute-start | bytes 442376 | tf_op jit(solution)/shard_map/ppermute | solution.py:774
  208.6 22.7 %collective-permute-start.34 = (bf16[832,384]{1,0:T(8,128)(2,1)S(1)}, bf16[832,384]{1,0:T(8,128)(2,1)S(1)}, u32[]{:S(2)}, u32[]{:S(2)}) collective-permute-start(bf16[832,384]{1,0:T(8,128)(2,1)S(1)} %get-tuple-element.158), channel_id=1, source_target_pairs={{0,4},{2,6},{4,0},{6,2},{8,12},{10,14},{12,8},{14,10},{16,20},{18,... | collective-permute-start | bytes 1916936 | tf_op jit(solution)/shard_map/ppermute | solution.py:774
  223.0 7.2 %collective-permute-start.45 = (bf16[48,1536]{1,0:T(8,128)(2,1)S(1)}, bf16[48,1536]{1,0:T(8,128)(2,1)S(1)}, u32[]{:S(2)}, u32[]{:S(2)}) collective-permute-start(bf16[48,1536]{1,0:T(8,128)(2,1)S(1)} %stage.49.refs_1_), channel_id=1, source_target_pairs={{0,16},{2,18},{4,20},{6,22},{8,24},{10,26},{12,28},{14,30},{16,0},... | collective-permute-start | bytes 442376 | tf_op jit(solution)/shard_map/ppermute | solution.py:774
  223.2 23.8 %collective-permute-start.53 = (bf16[384,768]{1,0:T(8,128)(2,1)S(1)}, bf16[384,768]{1,0:T(8,128)(2,1)S(1)}, u32[]{:S(2)}, u32[]{:S(2)}) collective-permute-start(bf16[384,768]{1,0:T(8,128)(2,1)S(1)} %stage.56.refs_1_), channel_id=1, source_target_pairs={{0,8},{2,10},{4,12},{6,14},{8,0},{10,2},{12,4},{14,6},{16,24},{18,... | collective-permute-start | bytes 1769480 | tf_op jit(solution)/shard_map/ppermute | solution.py:774
  230.2 16.2 %collective-permute-start.46 = (bf16[96,1536]{1,0:T(8,128)(2,1)S(1)}, bf16[96,1536]{1,0:T(8,128)(2,1)S(1)}, u32[]{:S(2)}, u32[]{:S(2)}) collective-permute-start(bf16[96,1536]{1,0:T(8,128)(2,1)S(1)} %stage.50.refs_1_), channel_id=1, source_target_pairs={{0,8},{2,10},{4,12},{6,14},{8,0},{10,2},{12,4},{14,6},{16,24},{18,... | collective-permute-start | bytes 884744 | tf_op jit(solution)/shard_map/ppermute | solution.py:774
  230.6 16.2 %collective-permute-start.27 = (bf16[384,384]{1,0:T(8,128)(2,1)S(1)}, bf16[384,384]{1,0:T(8,128)(2,1)S(1)}, u32[]{:S(2)}, u32[]{:S(2)}) collective-permute-start(bf16[384,384]{1,0:T(8,128)(2,1)S(1)} %get-tuple-element.152), channel_id=1, source_target_pairs={{0,4},{2,6},{4,0},{6,2},{8,12},{10,14},{12,8},{14,10},{16,20},{18,... | collective-permute-start | bytes 884744 | tf_op jit(solution)/shard_map/ppermute | solution.py:774
  231.3 58.8 %collective-permute-start.8 = (bf16[1024,384]{1,0:T(8,128)(2,1)}, bf16[1024,384]{1,0:T(8,128)(2,1)}, u32[]{:S(2)}, u32[]{:S(2)}) collective-permute-start(bf16[1024,384]{1,0:T(8,128)(2,1)} %get-tuple-element.110), channel_id=1, source_target_pairs={{0,1},{1,0},{2,3},{3,2},{4,5},{5,4},{6,7},{7,6},{8,9},{9,8},{10,11... | collective-permute-start | bytes 2359304 | tf_op jit(solution)/shard_map/ppermute | solution.py:770
  231.6 17.6 %collective-permute-start.35 = (bf16[416,384]{1,0:T(8,128)(2,1)S(1)}, bf16[416,384]{1,0:T(8,128)(2,1)S(1)}, u32[]{:S(2)}, u32[]{:S(2)}) collective-permute-start(bf16[416,384]{1,0:T(8,128)(2,1)S(1)} %get-tuple-element.160), channel_id=1, source_target_pairs={{0,2},{2,0},{4,6},{6,4},{8,10},{10,8},{12,14},{14,12},{16,18},{18,... | collective-permute-start | bytes 958472 | tf_op jit(solution)/shard_map/ppermute | solution.py:774
  246.5 30.0 %collective-permute-start.47 = (bf16[192,1536]{1,0:T(8,128)(2,1)S(1)}, bf16[192,1536]{1,0:T(8,128)(2,1)S(1)}, u32[]{:S(2)}, u32[]{:S(2)}) collective-permute-start(bf16[192,1536]{1,0:T(8,128)(2,1)S(1)} %stage.51.refs_1_), channel_id=1, source_target_pairs={{0,2},{2,0},{4,6},{6,4},{8,10},{10,8},{12,14},{14,12},{16,18},{18,... | collective-permute-start | bytes 1769480 | tf_op jit(solution)/shard_map/ppermute | solution.py:774
  246.9 7.2 %collective-permute-start.28 = (bf16[192,384]{1,0:T(8,128)(2,1)S(1)}, bf16[192,384]{1,0:T(8,128)(2,1)S(1)}, u32[]{:S(2)}, u32[]{:S(2)}) collective-permute-start(bf16[192,384]{1,0:T(8,128)(2,1)S(1)} %get-tuple-element.154), channel_id=1, source_target_pairs={{0,8},{2,10},{4,12},{6,14},{8,0},{10,2},{12,4},{14,6},{16,24},{18,... | collective-permute-start | bytes 442376 | tf_op jit(solution)/shard_map/ppermute | solution.py:774
  247.3 68.7 %collective-permute-start.54 = (bf16[768,768]{1,0:T(8,128)(2,1)S(1)}, bf16[768,768]{1,0:T(8,128)(2,1)}, u32[]{:S(2)}, u32[]{:S(2)}) collective-permute-start(bf16[768,768]{1,0:T(8,128)(2,1)S(1)} %stage.57.refs_1_), channel_id=1, source_target_pairs={{0,2},{2,0},{4,6},{6,4},{8,10},{10,8},{12,14},{14,12},{16,18},{18,... | collective-permute-start | bytes 3538952 | tf_op jit(solution)/shard_map/ppermute | solution.py:774
  249.3 15.2 %collective-permute-start.36 = (bf16[208,384]{1,0:T(8,128)(2,1)S(1)}, bf16[208,384]{1,0:T(8,128)(2,1)S(1)}, u32[]{:S(2)}, u32[]{:S(2)}) collective-permute-start(bf16[208,384]{1,0:T(8,128)(2,1)S(1)} %get-tuple-element.162), channel_id=1, source_target_pairs={{0,8},{2,10},{4,12},{6,14},{8,0},{10,2},{12,4},{14,6},{16,24},{18,... | collective-permute-start | bytes 479240 | tf_op jit(solution)/shard_map/ppermute | solution.py:774
  254.2 9.2 %collective-permute-start.29 = (bf16[96,384]{1,0:T(8,128)(2,1)S(1)}, bf16[96,384]{1,0:T(8,128)(2,1)S(1)}, u32[]{:S(2)}, u32[]{:S(2)}) collective-permute-start(bf16[96,384]{1,0:T(8,128)(2,1)S(1)} %get-tuple-element.156), channel_id=1, source_target_pairs={{0,16},{2,18},{4,20},{6,22},{8,24},{10,26},{12,28},{14,30},{16,0},... | collective-permute-start | bytes 221192 | tf_op jit(solution)/shard_map/ppermute | solution.py:774
  263.5 60.6 %collective-permute-start.25 = (f32[1024,384]{1,0:T(8,128)S(1)}, f32[1024,384]{1,0:T(8,128)}, u32[]{:S(2)}, u32[]{:S(2)}) collective-permute-start(f32[1024,384]{1,0:T(8,128)S(1)} %get-tuple-element.149), channel_id=1, source_target_pairs={{0,1},{1,0},{2,3},{3,2},{4,5},{5,4},{6,7},{7,6},{8,9},{9,8},{10,11... | collective-permute-start | bytes 4718600 | tf_op jit(solution)/shard_map/ppermute | solution.py:770
  264.6 6.2 %collective-permute-start.30 = (bf16[96,384]{1,0:T(8,128)(2,1)S(1)}, bf16[96,384]{1,0:T(8,128)(2,1)S(1)}, u32[]{:S(2)}, u32[]{:S(2)}) collective-permute-start(bf16[96,384]{1,0:T(8,128)(2,1)S(1)} %stage.36.refs_1_), channel_id=1, source_target_pairs={{0,16},{2,18},{4,20},{6,22},{8,24},{10,26},{12,28},{14,30},{16,0},... | collective-permute-start | bytes 221192 | tf_op jit(solution)/shard_map/ppermute | solution.py:774
  270.8 5.7 %collective-permute-start.37 = (bf16[104,384]{1,0:T(8,128)(2,1)S(1)}, bf16[104,384]{1,0:T(8,128)(2,1)S(1)}, u32[]{:S(2)}, u32[]{:S(2)}) collective-permute-start(bf16[104,384]{1,0:T(8,128)(2,1)S(1)} %get-tuple-element.164), channel_id=1, source_target_pairs={{0,16},{2,18},{4,20},{6,22},{8,24},{10,26},{12,28},{14,30},{16,0},... | collective-permute-start | bytes 239624 | tf_op jit(solution)/shard_map/ppermute | solution.py:774
  276.4 7.1 %collective-permute-start.31 = (bf16[192,384]{1,0:T(8,128)(2,1)S(1)}, bf16[192,384]{1,0:T(8,128)(2,1)S(1)}, u32[]{:S(2)}, u32[]{:S(2)}) collective-permute-start(bf16[192,384]{1,0:T(8,128)(2,1)S(1)} %stage.37.refs_1_), channel_id=1, source_target_pairs={{0,8},{2,10},{4,12},{6,14},{8,0},{10,2},{12,4},{14,6},{16,24},{18,... | collective-permute-start | bytes 442376 | tf_op jit(solution)/shard_map/ppermute | solution.py:774
  276.5 6.1 %collective-permute-start.38 = (bf16[104,384]{1,0:T(8,128)(2,1)S(1)}, bf16[104,384]{1,0:T(8,128)(2,1)S(1)}, u32[]{:S(2)}, u32[]{:S(2)}) collective-permute-start(bf16[104,384]{1,0:T(8,128)(2,1)S(1)} %stage.43.refs_1_), channel_id=1, source_target_pairs={{0,16},{2,18},{4,20},{6,22},{8,24},{10,26},{12,28},{14,30},{16,0},... | collective-permute-start | bytes 239624 | tf_op jit(solution)/shard_map/ppermute | solution.py:774
  282.6 37.3 %collective-permute-start.48 = (bf16[384,1536]{1,0:T(8,128)(2,1)}, bf16[384,1536]{1,0:T(8,128)(2,1)}, u32[]{:S(2)}, u32[]{:S(2)}) collective-permute-start(bf16[384,1536]{1,0:T(8,128)(2,1)} %stage.52.refs_1_), channel_id=1, source_target_pairs={{0,4},{2,6},{4,0},{6,2},{8,12},{10,14},{12,8},{14,10},{16,20},{18,... | collective-permute-start | bytes 3538952 | tf_op jit(solution)/shard_map/ppermute | solution.py:774
  288.9 25.8 %collective-permute-start.32 = (bf16[384,384]{1,0:T(8,128)(2,1)S(1)}, bf16[384,384]{1,0:T(8,128)(2,1)S(1)}, u32[]{:S(2)}, u32[]{:S(2)}) collective-permute-start(bf16[384,384]{1,0:T(8,128)(2,1)S(1)} %stage.38.refs_1_), channel_id=1, source_target_pairs={{0,4},{2,6},{4,0},{6,2},{8,12},{10,14},{12,8},{14,10},{16,20},{18,... | collective-permute-start | bytes 884744 | tf_op jit(solution)/shard_map/ppermute | solution.py:774
  290.1 24.8 %collective-permute-start.40 = (bf16[416,384]{1,0:T(8,128)(2,1)S(1)}, bf16[416,384]{1,0:T(8,128)(2,1)S(1)}, u32[]{:S(2)}, u32[]{:S(2)}) collective-permute-start(bf16[416,384]{1,0:T(8,128)(2,1)S(1)} %stage.45.refs_1_), channel_id=1, source_target_pairs={{0,2},{2,0},{4,6},{6,4},{8,10},{10,8},{12,14},{14,12},{16,18},{18,... | collective-permute-start | bytes 958472 | tf_op jit(solution)/shard_map/ppermute | solution.py:774
  314.8 14.1 %collective-permute-start.33 = (bf16[768,384]{1,0:T(8,128)(2,1)S(1)}, bf16[768,384]{1,0:T(8,128)(2,1)S(1)}, u32[]{:S(2)}, u32[]{:S(2)}) collective-permute-start(bf16[768,384]{1,0:T(8,128)(2,1)S(1)} %stage.39.refs_1_), channel_id=1, source_target_pairs={{0,2},{2,0},{4,6},{6,4},{8,10},{10,8},{12,14},{14,12},{16,18},{18,... | collective-permute-start | bytes 1769480 | tf_op jit(solution)/shard_map/ppermute | solution.py:774
  315.1 13.9 %collective-permute-start.41 = (bf16[832,384]{1,0:T(8,128)(2,1)S(1)}, bf16[832,384]{1,0:T(8,128)(2,1)S(1)}, u32[]{:S(2)}, u32[]{:S(2)}) collective-permute-start(bf16[832,384]{1,0:T(8,128)(2,1)S(1)} %stage.46.refs_3_), channel_id=1, source_target_pairs={{0,4},{2,6},{4,0},{6,2},{8,12},{10,14},{12,8},{14,10},{16,20},{18,... | collective-permute-start | bytes 1916936 | tf_op jit(solution)/shard_map/ppermute | solution.py:774
  (55 other events, 369.4 us)
where the time goes:
time: 339 us; the launch traced here: 334 us
  Pallas kernels  166 us (49%)
  waiting for transfers between devices  115 us (34%)
  starting transfers between devices  37.8 us (11%)
  local copies, waits for them, and re-layouts  12 us (4%)
    pallas_call x51, Pallas kernels, call(): pl.pallas_call(body, grid_spec=pltpu.PrefetchScalarGridSpec(num_scalar_pr...  166 us
    ppermute x38, waiting for transfers between devices, across(): return lax.ppermute(x, 'dp', [(i, i ^ mask) for i in range(size)])  112 us
    ppermute x38, starting transfers between devices, across(): return lax.ppermute(x, 'dp', [(i, i ^ mask) for i in range(size)])  34 us
    unnamed x103, local copies, waits for them, and re-layouts  9.34 us
  transfers between devices with their start and end apart: 55, of which 19 were waited for; matrix products, arithmetic and copies ran while one was open for 0% of the time, Pallas kernels for 37%

commit v1 on v0

--- a/solution.py
+++ b/solution.py
@@ -32,6 +32,11 @@
 
 
 ORDER = []
+
+VMEM = {
+    "their_rows": 6, "both_rows": 10, "vectors": 4, "qkv": 20, "attend": 18, "contrast": 20, "down_own": 20,
+    "last_halves": 20, "stage": 18, "up_end": 12, "down_end": 12, "last_end": 20, "attend_back": 24, "qkv_last": 24,
+}
 
 MICROS = {
     "their_rows": 2, "both_rows": 2, "vectors": 1, "qkv": 5, "pooled": 9, "attend": 11, "ffn": 25, "contrast": 6, "down_back": 9,
@@ -91,7 +96,7 @@
             scratch_shapes=list(scratch),
         ),
         out_shape=[jax.ShapeDtypeStruct(s, d) for s, d, _, _ in outs],
-        compiler_params=pltpu.CompilerParams(vmem_limit_bytes=vmem << 20),
+        compiler_params=pltpu.CompilerParams(vmem_limit_bytes=VMEM.get(name, vmem) << 20),
         cost_estimate=pl.CostEstimate(flops=int(MICROS[name] * 1.15e9), bytes_accessed=1000, transcendentals=0),
         input_output_aliases={n_scalars + i: o for i, o in (aliases or {}).items()},
         name=name,
@@ -366,7 +371,7 @@
 def ffn_kernel(
     count, me_ref, cls_ref, pair_ref, ctx_ref, x_ref, ow_here, ow_there, keep1_mine, keep1_theirs, uw_here, uw_there, dw_here,
     dw_there, up_b, feats, keep_mine, keep_theirs, res_ref, low_ref, act_ref, slope_ref, mixed_ref, mine_ref,
-    theirs_ref, pooled_ref, keep, value_buf,
+    theirs_ref, pooled_ref, keep, keep2, value_buf,
 ):
     step = pl.program_id(0)
     length = low_ref.shape[0]
@@ -382,6 +387,11 @@
             residual = x_ref[rows, :].astype(f32) + (branch + feats[0:1, :]) * (keep[...] * (1 / 0.9))
             res_ref[rows, :] = residual
             low_ref[rows, :] = (norm(residual)[0] * feats[1:2, :] + feats[2:3, :]).astype(bf16)
+
+    @pl.when(step < length // BLOCK)
+    def _():
+        rows = pl.ds(pl.multiple_of(step * BLOCK, BLOCK), BLOCK)
+        put_halves(keep2.at[rows, :], me_ref[0], keep_mine[...], keep_theirs[...])
 
     def run(up, down):
         def go():
@@ -418,9 +428,8 @@
         pooled = numbers.astype(f32)
         for r in range(length // BLOCK):
             rows = slice(r * BLOCK, (r + 1) * BLOCK)
-            put_halves(keep, me, keep_mine[rows, :].astype(f32), keep_theirs[rows, :])
             hidden = norm(res_ref[rows, :])[0] * feats[1:2, :] + feats[2:3, :]
-            mixed = hidden + (mixed_ref[rows, :] + feats[3:4, :]) * (keep[...] * (1 / 0.9))
+            mixed = hidden + (mixed_ref[rows, :] + feats[3:4, :]) * (keep2[rows, :].astype(f32) * (1 / 0.9))
             mixed_ref[rows, :] = mixed
             value_buf[...] = (norm(mixed)[0] * feats[4:5, :] + feats[5:6, :]).astype(bf16)
             here = lax.broadcasted_iota(jnp.int32, (16, BLOCK), 1) + r * BLOCK
@@ -435,6 +444,8 @@
     half = width // 2
     count = uw_here.shape[1] // UNITS
     units = 2 * uw_here.shape[1]
+    bands = length // BLOCK
+    assert bands <= 2 * count
     first = lambda i: jnp.minimum(i, count - 1)
     second = lambda i: jnp.maximum(i - count, 0)
     return call(
@@ -452,8 +463,8 @@
             (dw_there, (UNITS, width), lambda i, m, c, p: (second(i), 0)),
             (up_b, (1, UNITS), lambda i, m, c, p: (0, i)),
             (feats, None, None),
-            (keep[0], (length, half), lambda i, m, c, p: (m[0], 0)),
-            (keep[1], None, None),
+            (keep[0], (BLOCK, half), lambda i, m, c, p: (m[0] * bands + jnp.minimum(i, bands - 1), 0)),
+            (keep[1], (BLOCK, half), lambda i, m, c, p: (jnp.minimum(i, bands - 1), 0)),
         ],
         [
             ((length, width), f32, None, None),
@@ -465,7 +476,7 @@
             ((length, half), bf16, None, None),
             ((16, width), bf16, None, None),
         ],
-        [pltpu.VMEM((BLOCK, width), f32), pltpu.VMEM((BLOCK, width), bf16)],
+        [pltpu.VMEM((BLOCK, width), f32), pltpu.VMEM((length, width), bf16), pltpu.VMEM((BLOCK, width), bf16)],
         vmem=36,
     )
 
@@ -781,7 +792,7 @@
         out[...] = buf[pl.ds(start, rows), :].astype(bf16)
 
 
-def last_halves_kernel(cuts, here_ref, gq_here, gq_got, go_here, go_got, *refs):
+def last_parts_kernel(bands, here_ref, gq_here, gq_got, go_here, go_got, *refs):
     *outs, buf = refs
     rows, cols = gq_here.shape
     buf[:rows, :] = gq_here[...].astype(f32) + gq_got[...].astype(f32)
@@ -791,22 +802,29 @@
         low = rows + side * half
         buf[low : low + half, :] = go_here[:, lanes].astype(f32) + go_got[:, lanes].astype(f32)
     low = 0
-    for n, (high, bit) in enumerate(cuts):
-        halves_out((here_ref[0] >> bit) & 1, buf, outs[2 * n : 2 * n + 2], low)
+    for high, (bit, width) in bands:
+        many = 1 << width
+        halves_out((here_ref[0] >> bit) & (many - 1), buf, outs[:many], low)
+        outs = outs[many:]
         low = high
 
 
-def last_halves(here, gq_here, gq_got, go_here, go_got, cuts):
+def last_parts(here, gq_here, gq_got, go_here, go_got, bands):
     rows, cols = gq_here.shape
     rows += 2 * go_here.shape[0]
-    lows = [0] + [high for high, _ in cuts[:-1]]
+    lows = [0] + [high for high, _ in bands[:-1]]
+    sizes = [((high - low) >> width, 1 << width) for low, (high, (_, width)) in zip(lows, bands)]
     outs = call(
-        functools.partial(last_halves_kernel, cuts), "last_halves", (1,), [here],
+        functools.partial(last_parts_kernel, bands), "last_halves", (1,), [here],
         [(x, None, None) for x in (gq_here, gq_got, go_here, go_got)],
-        [(((high - low) // 2, cols), bf16, None, None) for low, (high, _) in zip(lows, cuts) for _ in range(2)],
+        [((n, cols), bf16, None, None) for n, many in sizes for _ in range(many)],
         [pltpu.VMEM((rows, cols), f32)],
     )
-    return [outs[2 * n : 2 * n + 2] for n in range(len(cuts))]
+    split = []
+    for _, many in sizes:
+        split.append(outs[:many])
+        outs = outs[many:]
+    return split
 
 
 def sum_of(refs):
@@ -817,41 +835,43 @@
 
 
 def stage_kernel(jobs, here_ref, *refs):
-    n_ins = sum(n for _, n, _, _ in jobs)
-    n_outs = sum(2 if kind == "fold" else 1 for kind, _, _, _ in jobs)
+    n_ins = sum(n for _, n, _ in jobs)
+    n_outs = sum(1 << step[1] if kind == "fold" else 1 for kind, _, step in jobs)
     ins, outs, bufs = list(refs[:n_ins]), list(refs[n_ins : n_ins + n_outs]), list(refs[n_ins + n_outs :])
-    for kind, n, bit, many in jobs:
+    for kind, n, step in jobs:
         parts, ins = ins[:n], ins[n:]
         if kind == "total":
             outs.pop(0)[...] = sum_of(parts).astype(bf16)
             continue
+        bit, many = step[0], 1 << step[1]
         at = (here_ref[0] >> bit) & (many - 1)
         buf = bufs.pop(0)
         if kind == "fold":
             buf[...] = sum_of(parts)
-            halves_out(at, buf, outs[:2])
-            outs = outs[2:]
+            halves_out(at, buf, outs[:many])
+            outs = outs[many:]
         else:
             place(buf, at, parts, 0)
             outs.pop(0)[...] = buf[...].astype(bf16)
 
 
-def stage(here, *jobs, free=False):
+def stage(here, *jobs, free=False, after=()):
     outs, scratch, counts = [], [], []
-    for kind, parts, _ in jobs:
+    for kind, parts, step in jobs:
         rows, cols = parts[0].shape
+        many = 1 << step[1] if kind == "fold" else 1
         if kind == "fold":
-            outs += [((rows // 2, cols), bf16, None, None)] * 2
+            outs += [((rows // many, cols), bf16, None, None)] * many
             scratch.append(pltpu.VMEM((rows, cols), f32))
         elif kind == "total":
             outs.append(((rows, cols), bf16, None, None))
         else:
             outs.append(((len(parts) * rows, cols), bf16, None, None))
             scratch.append(pltpu.VMEM((len(parts) * rows, cols), f32))
-        counts.append(2 if kind == "fold" else 1)
+        counts.append(many)
     results = call(
-        functools.partial(stage_kernel, [(kind, len(parts), bit, len(parts)) for kind, parts, bit in jobs]), "stage",
-        (1,), [here], [(p, None, None) for _, parts, _ in jobs for p in parts], outs, scratch, free=free,
+        functools.partial(stage_kernel, [(kind, len(parts), step) for kind, parts, step in jobs]), "stage", (1,),
+        [here], [(p, None, None) for _, parts, _ in jobs for p in parts], outs, scratch, free=free, after=after,
     )
     split = []
     for n in counts:
@@ -861,44 +881,42 @@
 
 
 class Chain:
-    def __init__(self, halves, order, size):
+    def __init__(self, parts, order, size):
         self.order, self.size, self.step = order, size, 0
-        self.parts = halves
-        self.send(halves[1])
-
-    def send(self, x):
-        bit = self.order[self.step]
-        self.parts = [self.parts[0], across(x, 1 << bit, self.size)]
+        self.last = len(order) - 1
+        self.end = 2 * self.last + 1
+        self.send(parts)
+
+    def now(self, step):
+        return self.order[step if step <= self.last else self.end - step]
+
+    def send(self, parts):
+        bit, _ = self.now(self.step)
+        self.parts = [parts[0]] + [across(x, m << bit, self.size) for m, x in enumerate(parts[1:], 1)]
 
     def job(self):
-        last = len(self.order) - 1
-        if self.step < last:
+        if self.step < self.last:
             return ("fold", self.parts, self.order[self.step + 1])
-        if self.step == last:
-            return ("total", self.parts, 0)
-        return ("join", self.parts, self.order[2 * last + 1 - self.step])
+        if self.step == self.last:
+            return ("total", self.parts, (0, 0))
+        return ("join", self.parts, self.now(self.step))
 
     def take(self, result):
-        last = len(self.order) - 1
         self.step += 1
-        if self.step <= last:
-            self.parts = result
-            bit, x = self.order[self.step], result[1]
-        else:
-            self.parts = [result, result]
-            bit, x = self.order[2 * last + 1 - self.step], result
-        self.parts = [self.parts[0], across(x, 1 << bit, self.size)]
-
-
-def advance(here, *chains, free=False):
-    for chain, result in zip(chains, stage(here, *[c.job() for c in chains], free=free)):
+        if self.step > self.last:
+            result = [result] * (1 << self.now(self.step)[1])
+        self.send(result)
+
+
+def advance(here, *chains, free=False, after=()):
+    for chain, result in zip(chains, stage(here, *[c.job() for c in chains], free=free, after=after)):
         chain.take(result)
 
 
-def plain_sum(at, halves):
-    whole = jnp.where(at == 0, jnp.stack(halves), jnp.stack(halves[::-1]))
+def plain_sum(at, parts):
+    whole = jnp.stack([lax.dynamic_index_in_dim(jnp.stack(parts), at ^ m, 0, False) for m in range(len(parts))])
     whole = lax.psum(whole, "dp")
-    return jnp.where(at == 0, whole, whole[::-1])
+    return [lax.dynamic_index_in_dim(whole, at ^ m, 0, False) for m in range(len(parts))]
 
 
 def place(buf, at, parts, low):
@@ -930,12 +948,14 @@
     )[0]
 
 
-def last_end_kernel(bits, here_ref, *refs):
-    *halves, qkv_ref, vec_ref, out_ref, buf = refs
+def last_end_kernel(steps, here_ref, *refs):
+    *parts, qkv_ref, vec_ref, out_ref, buf = refs
     low = 0
-    for n, bit in enumerate(bits):
-        place(buf, (here_ref[0] >> bit) & 1, halves[2 * n : 2 * n + 2], low)
-        low += 2 * halves[2 * n].shape[0]
+    for bit, width in steps:
+        many = 1 << width
+        place(buf, (here_ref[0] >> bit) & (many - 1), parts[:many], low)
+        low += many * parts[0].shape[0]
+        parts = parts[many:]
     rows, cols = qkv_ref.shape[1:]
     for c in range(3):
         qkv_ref[c] = buf[c * rows : (c + 1) * rows, :]
@@ -946,11 +966,11 @@
         out_ref[:, side * cols : side * cols + cols] = buf[low + side * half : low + (side + 1) * half, :]
 
 
-def last_end(here, bands, bits, half):
-    rows = sum(2 * b[0].shape[0] for b in bands)
+def last_end(here, bands, steps, half):
+    rows = sum(len(b) * b[0].shape[0] for b in bands)
     cols = bands[0][0].shape[1]
     return call(
-        functools.partial(last_end_kernel, bits), "last_end", (1,), [here], [(q, None, None) for b in bands for q in b],
+        functools.partial(last_end_kernel, steps), "last_end", (1,), [here], [(q, None, None) for b in bands for q in b],
         [((3, 2 * cols, cols), f32, None, None), ((16, cols), f32, None, None), ((half, 2 * cols), f32, None, None)],
         [pltpu.VMEM((rows, cols), f32)],
         free=True,
@@ -1129,8 +1149,8 @@
         near = [pooled] + [across(pooled, m, dp_size) for m in (1, 2, 3)]
     go_there = other(their_rows(me_one, [grad_out], length)[0])
     if quick:
-        (near,) = stage(here_one, ("join", near, 0))
-        (all_here,) = stage(here_one, ("join", [near] + [across(near, m, dp_size) for m in (4, 8, 12)], 2))
+        (near,) = stage(here_one, ("join", near, (0, 2)))
+        (all_here,) = stage(here_one, ("join", [near] + [across(near, m, dp_size) for m in (4, 8, 12)], (2, 2)))
         all_there = other(all_here)
     pool_rows = cls.shape[0]
     rank = here * 2 + me
@@ -1164,10 +1184,10 @@
     part, bias_there, gu_there = up_back(bit1, low, g, slope, up_there, down_there, False)
     down = down_own(bit0, act, g, other(gd_there))
     if quick:
-        down = Chain(down, (0, 2, 3, 1), dp_size)
+        down = Chain(down, ((0, 1), (1, 1), (2, 1), (3, 1)), dp_size)
     part, bias_here, *up = up_back(bit1, low, g, slope, up_weight, down_weight, True, part, other(gu_there))
     if quick:
-        up = Chain(up, (1, 0, 2, 3), dp_size)
+        up = Chain(up, ((1, 1), (0, 1), (2, 1), (3, 1)), dp_size)
     gr, grad_ctx, delta, sums1, go_there, go_here = out_back(
         me_one, gm, part, res, ctx, keep1, out_weight, out_there, feats, []
     )
@@ -1179,26 +1199,39 @@
         advance(here_one, down, up)
     gq_there, gq_here = qkv_last(me_one, x, grads, bias_here, bias_there, sums1, sums2)
     rows = gq_here.shape[0] + D
-    cuts = ((rows // 256 * 128, 0), (rows, 1))
-    last = last_halves(here_one, gq_here, other(gq_there), go_here, go_got, cuts)
+    orders = [((0, 1), (1, 1), (2, 1), (3, 1)), ((1, 1), (0, 1), (2, 1), (3, 1))]
+    firsts = [order[0] for order in orders]
+    last = last_parts(
+        here_one, gq_here, other(gq_there), go_here, go_got, list(zip([rows // 256 * 128, rows], firsts))
+    )
     if quick:
-        orders = ((0, 1, 2, 3), (1, 0, 2, 3))
-        last = [Chain(halves, order, dp_size) for halves, order in zip(last, orders)]
+        last = [Chain(parts, order, dp_size) for parts, order in zip(last, orders)]
     gt_mine, gt_theirs = tokens_back(me_one, gr, grads, qkv_weight, qkv_there)
     if quick:
-        while any(chain.step < 7 for chain in (down, up, *last)):
-            for chain in (*last, down, up):
-                if chain.step < 7:
-                    advance(here_one, chain, free=True)
+        marks = [last[0].parts[0]]
+        for c in last:
+            advance(here_one, c, free=True, after=[gt_mine])
+        marks.append(last[0].parts[0])
+        while any(c.step < c.end for c in last):
+            for c in last:
+                advance(here_one, c, free=True)
+            marks.append(last[0].parts[0])
+        for chain, waits in ((down, [1]), (up, [1])):
+            for wait in waits:
+                if chain.step < chain.end:
+                    after = [marks[min(wait, len(marks) - 1)]] if wait >= 0 else []
+                    advance(here_one, chain, free=True, after=after)
+            while chain.step < chain.end:
+                advance(here_one, chain, free=True)
         down, up = down.parts, up.parts
         last = [chain.parts for chain in last]
     else:
         down, up = plain_sum(bit0[0], down), plain_sum(bit1[0], up)
-        last = [plain_sum((here >> bit) & 1, halves) for halves, (_, bit) in zip(last, cuts)]
+        last = [plain_sum((here >> bit) & ((1 << width) - 1), parts) for parts, (bit, width) in zip(last, firsts)]
     grad_tokens = both_rows(me_one, gt_mine, other(gt_theirs))
     g_down_w = end(bit0, down, "down_end")
     g_up_w = end(bit1, up, "up_end")
-    g_qkv_w, vec_sum, g_out_w = last_end(here_one, last, (0, 1), half)
+    g_qkv_w, vec_sum, g_out_w = last_end(here_one, last, firsts, half)
     n_up = units // half
     return (
         layer_out,

time: 339 us -> 335 us (0.988)
  waiting for transfers between devices: 115 us -> 84 us
  starting transfers between devices: 37.8 us -> 57.2 us
  local copies, waits for them, and re-layouts: 12 us -> 16.2 us
  Pallas kernels: 166 us -> 170 us
    ppermute x38, waiting for transfers between devices: 112 us -> 77.9 us  [across(): return lax.ppermute(x, 'dp', [(i, i ^ mask) for i in range(size)])]
    ppermute x38, starting transfers between devices: 34 us -> 53 us  [across(): return lax.ppermute(x, 'dp', [(i, i ^ mask) for i in range(size)])]
    pallas_call x51, Pallas kernels: 166 us -> 170 us  [call(): pl.pallas_call(body, grid_spec=pltpu.PrefetchScalarGridSpec(num_scalar_pr...]
    unnamed x103 -> x107, local copies, waits for them, and re-layouts: 9.34 us -> 13.6 us
    ppermute x17, waiting for transfers between devices: 2.75 us -> 6.17 us  [other(): return lax.ppermute(x, 'tensor', SWAP)]
  transfers between devices with their start and end apart: 55 -> 55, of which waited for: 19 -> 24; matrix products, arithmetic and copies ran while one was open for 0% -> 1% of each run, Pallas kernels for 37% -> 38%
where the time goes in v1:
time: 335 us; the launch traced here: 330 us
  Pallas kernels  170 us (51%)
  waiting for transfers between devices  84 us (25%)
  starting transfers between devices  57.2 us (17%)
  local copies, waits for them, and re-layouts  16.2 us (5%)
    pallas_call x51, Pallas kernels, call(): pl.pallas_call(body, grid_spec=pltpu.PrefetchScalarGridSpec(num_scalar_pr...  170 us
    ppermute x38, waiting for transfers between devices, across(): return lax.ppermute(x, 'dp', [(i, i ^ mask) for i in range(size)])  77.9 us
    ppermute x38, starting transfers between devices, across(): return lax.ppermute(x, 'dp', [(i, i ^ mask) for i in range(size)])  53 us
    unnamed x107, local copies, waits for them, and re-layouts  13.6 us
  transfers between devices with their start and end apart: 55, of which 24 were waited for; matrix products, arithmetic and copies ran while one was open for 1% of the time, Pallas kernels for 38%

profile of v1, /device:TPU:0, one launch (start us, length us, event | category | flops | bytes accessed | tf_op | source)
XLA Modules:
  0.0 330.4 jit_solution(13549197629772599089)
XLA Ops:
  1.3 2.1 their_rows.3.refs_3_
  6.9 7.2 %qkv.1 = (bf16[1024,768]{1,0:T(8,128)(2,1)S(1)}, bf16[1024,768]{1,0:T(8,128)(2,1)S(1)}, bf16[1024,768]{1,0:T(8,128)(2,1)S(1)}, bf16[1024,768]{1,0:T(8,128)(2,1)S(1)}) custom-call(s32[1]{0:T(128)} %bitcast.refs_0_.refs_1_, bf16[2048,384]{1,0:T(8,128)(2,1)} %refs_1_.5, bf16[1024,384]{1,0:T(8,128)(2,1)} %collective-permute-done.refs_2_, ...), custom_call_target="tpu_custom_call" | custom-call | flops 5750000128 | bytes 1000 | tf_op jit(solution)/shard_map/qkv/pallas_call | solution.py:88
  14.1 4.1 %their_rows.4 = (bf16[1024,384]{1,0:T(8,128)(2,1)S(1)}, bf16[1024,384]{1,0:T(8,128)(2,1)S(1)}) custom-call(s32[1]{0:T(128)} %bitcast.refs_0_.refs_1_, s32[2048,384]{1,0:T(8,128)} %refs_5_.6, s32[2048,384]{1,0:T(8,128)} %refs_7_.4, bf16[1024,768]{1,0:T(8,128)(2,1)S(1)} %get-tuple-element.102.refs_3_.refs_4_.refs_1_), custom_call_target="tpu_custom_call" | custom-call | flops 2300000000 | bytes 1000 | tf_op jit(solution)/shard_map/their_rows/pallas_call | solution.py:88
  19.1 14.7 %attend.1 = (bf16[1024,768]{1,0:T(8,128)(2,1)S(1)}, f32[16,1024]{1,0:T(8,128)S(1)}) custom-call(s32[1024]{0:T(1024)} %bitcast.11, s32[1024,128]{1,0:T(8,128)S(1)} %broadcast_in_dim.12.refs_1_, s32[1,1024]{1,0:T(1,128)} %copy-done.37, bf16[1024,768]{1,0:T(8,128)(2,1)} %copy-done.21, bf16[1024,768]{1,0:T(8,128)(2,1)S(1)} %get-tuple-element.100.refs_4_, ...), custom_call_target="tpu_custom_call" | custom-call | flops 12650000384 | bytes 1000 | tf_op jit(solution)/shard_map/attend/pallas_call | solution.py:88
  34.8 26.1 %ffn.1 = (f32[1024,768]{1,0:T(8,128)S(1)}, bf16[1024,768]{1,0:T(8,128)(2,1)S(1)}, bf16[1024,3072]{1,0:T(8,128)(2,1)}, bf16[1024,3072]{1,0:T(8,128)(2,1)}, f32[10...) custom-call(s32[1]{0:T(128)} %bitcast.refs_0_.refs_1_, ...), custom_call_target="tpu_custom_call" | custom-call | flops 28750000128 | bytes 1000 | tf_op jit(solution)/shard_map/ffn/pallas_call | solution.py:88
  64.6 2.1 collective-permute-start.9
  68.9 2.6 their_rows.5.refs_5_
  73.0 2.4 collective-permute-start.12
  75.4 1.8 collective-permute-start.13
  79.0 5.3 %collective-permute-done.13.refs_3_ = bf16[64,768]{1,0:T(8,128)(2,1)S(1)} collective-permute-done((bf16[64,768]{1,0:T(8,128)(2,1)S(1)}, bf16[64,768]{1,0:T(8,128)(2,1)S(1)}, u32[]{:S(2)}, u32[]{:S(2)}) %collective-permute-start.13) | collective-permute-done | bytes 98336 | tf_op jit(solution)/shard_map/ppermute | solution.py:785
  86.4 7.2 %contrast.1 = (f32[384,768]{1,0:T(8,128)}, f32[1,768]{1,0:T(1,128)S(1)}, f32[8,768]{1,0:T(8,128)S(1)}, f32[8,128]{1,0:T(8,128)S(1)}) custom-call(s32[1]{0:T(128)} %bitcast.3.refs_0_, s32[1]{0:T(128)} %bitcast.refs_0_.refs_1_, bf16[256,768]{1,0:T(8,128)(2,1)S(1)} %stage.30.refs_2_.refs_8_, bf16[256,768]{1,0:T(8,128)(2,1)} %collective-permute-done.15.refs_3_, ...), custom_call_target="tpu_custom_call" | custom-call | flops 6899999744 | bytes 1000 | tf_op jit(solution)/shard_map/contrast/pallas_call | solution.py:88
  93.6 9.2 %down_back.1 = (bf16[1024,768]{1,0:T(8,128)(2,1)S(1)}, f32[1024,768]{1,0:T(8,128)S(1)}, f32[8,768]{1,0:T(8,128)S(1)}, bf16[1536,768]{1,0:T(8,128)(2,1)S(1)}) custom-call(s32[1]{0:T(128)} %bitcast.refs_0_.refs_1_, s32[8]{0:T(128)S(1)} %dynamic-slice_bitcast_fusion.refs_1_, f32[1024,768]{1,0:T(8,128)S(1)} %copy-done.29, bf16[2048,384]{1,0:T(8,128)(2,1)} %refs_3_.3, ...), custom_call_target="tpu_custom_call" | custom-call | flops 10350000128 | bytes 1000 | tf_op jit(solution)/shard_map/down_back/pallas_call | solution.py:88
  103.0 10.5 %up_back.1 = (f32[1024,768]{1,0:T(8,128)S(1)}, f32[1,1536]{1,0:T(1,128)S(1)}, bf16[768,1536]{1,0:T(8,128)(2,1)S(1)}) custom-call(s32[1]{0:T(128)S(6)} %and.8.refs_0_, bf16[1024,768]{1,0:T(8,128)(2,1)S(1)} %copy-done.31, bf16[1024,768]{1,0:T(8,128)(2,1)S(1)} %get-tuple-element.119.refs_2_, bf16[1024,3072]{1,0:T(8,128)(2,1)} %get-tuple-element.120.refs_3_, ...), custom_call_target="tpu_custom_call" | custom-call | flops 11500000256 | bytes 1000 | tf_op jit(solution)/shard_map/up_back/pallas_call | solution.py:88
  115.4 5.1 %down_own.1 = (bf16[768,768]{1,0:T(8,128)(2,1)S(1)}, bf16[768,768]{1,0:T(8,128)(2,1)S(1)}) custom-call(s32[1]{0:T(128)S(6)} %and.9.refs_0_, bf16[1024,3072]{1,0:T(8,128)(2,1)} %get-tuple-element.115.refs_9_.refs_1_, bf16[1024,768]{1,0:T(8,128)(2,1)S(1)} %get-tuple-element.119.refs_2_, bf16[1536,768]{1,0:T(8,128)(2,1)} %copy-done.48, ...), custom_call_target="tpu_custom_call" | custom-call | flops 4024999936 | bytes 1000 | tf_op jit(solution)/shard_map/down_own/pallas_call | solution.py:88
  122.6 11.2 %up_own.1 = (f32[1024,768]{1,0:T(8,128)S(1)}, f32[1,1536]{1,0:T(1,128)S(1)}, bf16[384,1536]{1,0:T(8,128)(2,1)S(1)}, bf16[384,1536]{1,0:T(8,128)(2,1)S(1)}) custom-call(s32[1]{0:T(128)S(6)} %and.8.refs_0_, bf16[1024,768]{1,0:T(8,128)(2,1)S(1)} %copy-done.31, bf16[1024,768]{1,0:T(8,128)(2,1)S(1)} %get-tuple-element.119.refs_2_, ...), custom_call_target="tpu_custom_call" | custom-call | flops 11500000256 | bytes 1000 | tf_op jit(solution)/shard_map/up_own/pallas_call | solution.py:88
  133.8 2.0 collective-permute-start.22
  135.7 9.2 %out_back.1 = (f32[1024,768]{1,0:T(8,128)S(1)}, bf16[1024,768]{1,0:T(8,128)(2,1)S(1)}, f32[16,1024]{1,0:T(8,128)S(1)}, f32[8,768]{1,0:T(8,128)S(1)}, bf16[384,76...) custom-call(s32[1]{0:T(128)} %bitcast.refs_0_.refs_1_, f32[1024,768]{1,0:T(8,128)S(1)} %get-tuple-element.117.refs_1_, ...), custom_call_target="tpu_custom_call" | custom-call | flops 10350000128 | bytes 1000 | tf_op jit(solution)/shard_map/out_back/pallas_call | solution.py:88
  146.1 2.5 collective-permute-done.20.refs_2_
  150.4 20.9 %attend_back.1 = (bf16[1024,768]{1,0:T(8,128)(2,1)S(1)}, bf16[1024,768]{1,0:T(8,128)(2,1)S(1)}, bf16[1024,768]{1,0:T(8,128)(2,1)S(1)}) custom-call(s32[1024]{0:T(1024)} %bitcast.12, s32[1024,128]{1,0:T(8,128)S(1)} %broadcast_in_dim.12.refs_1_, s32[1,1024]{1,0:T(1,128)} %copy-done.37, bf16[1024,768]{1,0:T(8,128)(2,1)} %copy-done.21, ...), custom_call_target="tpu_custom_call" | custom-call | flops 24149999616 | bytes 1000 | tf_op jit(solution)/shard_map/attend_back/pallas_call | solution.py:88
  171.4 3.0 collective-permute-done.21.refs_2_
  175.8 4.1 %qkv_last.1 = (bf16[2432,384]{1,0:T(8,128)(2,1)S(1)}, bf16[2432,384]{1,0:T(8,128)(2,1)S(1)}) custom-call(s32[1]{0:T(128)} %bitcast.refs_0_.refs_1_, bf16[1024,768]{1,0:T(8,128)(2,1)S(1)} %copy-done.17, bf16[1024,768]{1,0:T(8,128)(2,1)S(1)} %get-tuple-element.136.refs_5_.refs_2_, bf16[1024,768]{1,0:T(8,128)(2,1)S(1)} %get-tuple-element.137.refs_3_, ...), custom_call_target="tpu_custom_call" | custom-call | flops 4600000000 | bytes 1000 | tf_op jit(solution)/shard_map/qkv_last/pallas_call | solution.py:88
  180.4 4.2 %collective-permute-done.24.refs_4_ = bf16[384,768]{1,0:T(8,128)(2,1)S(1)} collective-permute-done((bf16[384,768]{1,0:T(8,128)(2,1)S(1)}, bf16[384,768]{1,0:T(8,128)(2,1)S(1)}, u32[]{:S(2)}, u32[]{:S(2)}) %collective-permute-start.24) | collective-permute-done | bytes 589856 | tf_op jit(solution)/shard_map/ppermute | solution.py:781
  189.3 1.7 collective-permute-start.34
  191.1 8.8 %tokens_back.1 = (f32[1024,384]{1,0:T(8,128)S(1)}, f32[1024,384]{1,0:T(8,128)}) custom-call(s32[1]{0:T(128)} %bitcast.refs_0_.refs_1_, f32[1024,768]{1,0:T(8,128)} %copy-done.19, bf16[1024,768]{1,0:T(8,128)(2,1)} %copy-done.2, bf16[1024,768]{1,0:T(8,128)(2,1)S(1)} %get-tuple-element.137.refs_3_, bf16[1024,768]{1,0:T(8,128)(2,1)S(1)} %get-tuple-element.138.refs_4_, ...), custom_call_target="tpu_custom_call" | custom-call | flops 5750000128 | bytes 1000 | tf_op jit(solution)/shard_map/tokens_back/pallas_call | solution.py:88
  199.9 2.0 collective-permute-done.26.refs_2_
  202.1 1.8 collective-permute-start.27
  204.1 2.5 collective-permute-start.50
  206.6 7.1 %collective-permute-done.42.refs_2_ = bf16[192,1536]{1,0:T(8,128)(2,1)S(1)} collective-permute-done((bf16[192,1536]{1,0:T(8,128)(2,1)S(1)}, bf16[192,1536]{1,0:T(8,128)(2,1)S(1)}, u32[]{:S(2)}, u32[]{:S(2)}) %collective-permute-start.42) | collective-permute-done | bytes 589856 | tf_op jit(solution)/shard_map/ppermute | solution.py:785
  220.6 7.0 %collective-permute-done.43.refs_2_ = bf16[96,1536]{1,0:T(8,128)(2,1)S(1)} collective-permute-done((bf16[96,1536]{1,0:T(8,128)(2,1)S(1)}, bf16[96,1536]{1,0:T(8,128)(2,1)S(1)}, u32[]{:S(2)}, u32[]{:S(2)}) %collective-permute-start.43) | collective-permute-done | bytes 294944 | tf_op jit(solution)/shard_map/ppermute | solution.py:785
  228.4 3.0 collective-permute-start.52
  233.3 3.0 collective-permute-done.44.refs_2_
  236.4 7.4 %collective-permute-done.29.refs_2_ = bf16[96,384]{1,0:T(8,128)(2,1)S(1)} collective-permute-done((bf16[96,384]{1,0:T(8,128)(2,1)S(1)}, bf16[96,384]{1,0:T(8,128)(2,1)S(1)}, u32[]{:S(2)}, u32[]{:S(2)}) %collective-permute-start.29) | collective-permute-done | bytes 73760 | tf_op jit(solution)/shard_map/ppermute | solution.py:785
  243.8 3.5 %collective-permute-start.30 = (bf16[96,384]{1,0:T(8,128)(2,1)S(1)}, bf16[96,384]{1,0:T(8,128)(2,1)S(1)}, u32[]{:S(2)}, u32[]{:S(2)}) collective-permute-start(bf16[96,384]{1,0:T(8,128)(2,1)S(1)} %stage.36.refs_1_), channel_id=1, source_target_pairs={{0,16},{2,18},{4,20},{6,22},{8,24},{10,26},{12,28},{14,30},{16,0},... | collective-permute-start | bytes 221192 | tf_op jit(solution)/shard_map/ppermute | solution.py:785
  247.6 2.9 collective-permute-start.46
  251.8 1.7 collective-permute-start.31
  255.3 1.8 collective-permute-start.53
  257.1 3.1 collective-permute-done.38.refs_2_
  260.3 3.0 collective-permute-start.39
  263.5 2.4 collective-permute-start.32
  266.8 8.8 %collective-permute-done.32.refs_2_ = bf16[384,384]{1,0:T(8,128)(2,1)S(1)} collective-permute-done((bf16[384,384]{1,0:T(8,128)(2,1)S(1)}, bf16[384,384]{1,0:T(8,128)(2,1)S(1)}, u32[]{:S(2)}, u32[]{:S(2)}) %collective-permute-start.32) | collective-permute-done | bytes 294944 | tf_op jit(solution)/shard_map/ppermute | solution.py:785
  278.9 8.5 %collective-permute-done.40.refs_2_ = bf16[416,384]{1,0:T(8,128)(2,1)S(1)} collective-permute-done((bf16[416,384]{1,0:T(8,128)(2,1)S(1)}, bf16[416,384]{1,0:T(8,128)(2,1)S(1)}, u32[]{:S(2)}, u32[]{:S(2)}) %collective-permute-start.40) | collective-permute-done | bytes 319520 | tf_op jit(solution)/shard_map/ppermute | solution.py:785
  295.0 3.8 %both_rows.2 = bf16[2048,384]{1,0:T(8,128)(2,1)} custom-call(s32[1]{0:T(128)} %bitcast.refs_0_.refs_1_, bf16[1024,384]{1,0:T(8,128)(2,1)} %copy-done.20, bf16[1024,384]{1,0:T(8,128)(2,1)} %collective-permute-done.8.refs_2_), custom_call_target="tpu_custom_call" | custom-call | flops 2300000000 | bytes 1000 | tf_op jit(solution)/shard_map/both_rows/pallas_call | solution.py:88
  298.8 4.9 %both_rows.3 = f32[2048,384]{1,0:T(8,128)} custom-call(s32[1]{0:T(128)} %bitcast.refs_0_.refs_1_, f32[1024,384]{1,0:T(8,128)} %copy-done.18, f32[1024,384]{1,0:T(8,128)} %collective-permute-done.25.refs_2_), custom_call_target="tpu_custom_call" | custom-call | flops 2300000000 | bytes 1000 | tf_op jit(solution)/shard_map/both_rows/pallas_call | solution.py:88
  303.7 2.1 collective-permute-done.41.refs_4_
  305.8 4.2 %last_end.1 = (f32[3,768,384]{2,1,0:T(8,128)}, f32[16,384]{1,0:T(8,128)S(1)}, f32[384,768]{1,0:T(8,128)}) custom-call(s32[1]{0:T(128)} %bitcast.4.refs_0_, bf16[768,384]{1,0:T(8,128)(2,1)} %stage.39.refs_1_, bf16[768,384]{1,0:T(8,128)(2,1)} %collective-permute-done.33.refs_2_, bf16[832,384]{1,0:T(8,128)(2,1)S(1)} %stage.46.refs_3_, ...), custom_call_target="tpu_custom_call" | custom-call | flops 3449999872 | bytes 1000 | tf_op jit(solution)/shard_map/last_end/pallas_call | solution.py:88
  311.7 11.3 %collective-permute-done.54.refs_2_ = bf16[768,768]{1,0:T(8,128)(2,1)S(1)} collective-permute-done((bf16[768,768]{1,0:T(8,128)(2,1)S(1)}, bf16[768,768]{1,0:T(8,128)(2,1)S(1)}, u32[]{:S(2)}, u32[]{:S(2)}) %collective-permute-start.54) | collective-permute-done | bytes 1179680 | tf_op jit(solution)/shard_map/ppermute | solution.py:785
  323.0 2.6 down_end.1
  326.0 4.2 %up_end.1 = f32[768,1536]{1,0:T(8,128)} custom-call(s32[1]{0:T(128)S(6)} %and.8.refs_0_, bf16[384,1536]{1,0:T(8,128)(2,1)} %stage.52.refs_1_, bf16[384,1536]{1,0:T(8,128)(2,1)} %collective-permute-done.48.refs_2_), custom_call_target="tpu_custom_call" | custom-call | flops 3449999872 | bytes 1000 | tf_op jit(solution)/shard_map/up_end/pallas_call | solution.py:88
  (235 shorter events, 57.7 us)
Async XLA Ops:
  0.7 6.2 %collective-permute-start.1 = (bf16[3,768,384]{2,1,0:T(8,128)(2,1)}, bf16[3,768,384]{2,1,0:T(8,128)(2,1)}, u32[]{:S(2)}, u32[]{:S(2)}) collective-permute-start(bf16[3,768,384]{2,1,0:T(8,128)(2,1)} %refs_5_.7), channel_id=1, source_target_pairs={{0,1},{1,0},{2,3},{3,2},{4,5},{5,4},{6,7},{7,6},{8,9},{9,8},{10,11... | collective-permute-start | bytes 5308424 | tf_op jit(solution)/shard_map/ppermute | solution.py:781
  3.5 30.3 %collective-permute-start.5 = (bf16[768,1536]{1,0:T(8,128)(2,1)}, bf16[768,1536]{1,0:T(8,128)(2,1)}, u32[]{:S(2)}, u32[]{:S(2)}) collective-permute-start(bf16[768,1536]{1,0:T(8,128)(2,1)} %refs_4_.3), channel_id=1, source_target_pairs={{0,1},{1,0},{2,3},{3,2},{4,5},{5,4},{6,7},{7,6},{8,9},{9,8},{10,11... | collective-permute-start | bytes 7077896 | tf_op jit(solution)/shard_map/ppermute | solution.py:781
  4.0 29.8 %collective-permute-start.6 = (bf16[1536,768]{1,0:T(8,128)(2,1)}, bf16[1536,768]{1,0:T(8,128)(2,1)}, u32[]{:S(2)}, u32[]{:S(2)}) collective-permute-start(bf16[1536,768]{1,0:T(8,128)(2,1)} %refs_5_.5), channel_id=1, source_target_pairs={{0,1},{1,0},{2,3},{3,2},{4,5},{5,4},{6,7},{7,6},{8,9},{9,8},{10,11... | collective-permute-start | bytes 7077896 | tf_op jit(solution)/shard_map/ppermute | solution.py:781
  6.1 27.6 %collective-permute-start.3 = (bf16[384,768]{1,0:T(8,128)(2,1)S(1)}, bf16[384,768]{1,0:T(8,128)(2,1)S(1)}, u32[]{:S(2)}, u32[]{:S(2)}) collective-permute-start(bf16[384,768]{1,0:T(8,128)(2,1)S(1)} %copy-done.7), channel_id=1, source_target_pairs={{0,1},{1,0},{2,3},{3,2},{4,5},{5,4},{6,7},{7,6},{8,9},{9,8},{10,11... | collective-permute-start | bytes 1769480 | tf_op jit(solution)/shard_map/ppermute | solution.py:781
  18.3 15.5 %collective-permute-start.4 = (bf16[1024,384]{1,0:T(8,128)(2,1)S(1)}, bf16[1024,384]{1,0:T(8,128)(2,1)S(1)}, u32[]{:S(2)}, u32[]{:S(2)}) collective-permute-start(bf16[1024,384]{1,0:T(8,128)(2,1)S(1)} %get-tuple-element.103.refs_6_), channel_id=1, source_target_pairs={{0,1},{1,0},{2,3},{3,2},{4,5},{5,4},{6,7},{7,6},{8,9},{9,8},{10,11... | collective-permute-start | bytes 2359304 | tf_op jit(solution)/shard_map/ppermute | solution.py:781
  18.7 15.1 %collective-permute-start.7 = (bf16[1024,384]{1,0:T(8,128)(2,1)S(1)}, bf16[1024,384]{1,0:T(8,128)(2,1)S(1)}, u32[]{:S(2)}, u32[]{:S(2)}) collective-permute-start(bf16[1024,384]{1,0:T(8,128)(2,1)S(1)} %get-tuple-element.107), channel_id=1, source_target_pairs={{0,1},{1,0},{2,3},{3,2},{4,5},{5,4},{6,7},{7,6},{8,9},{9,8},{10,11... | collective-permute-start | bytes 2359304 | tf_op jit(solution)/shard_map/ppermute | solution.py:781
  64.6 6.9 %collective-permute-start.9 = (bf16[16,768]{1,0:T(8,128)(2,1)S(1)}, bf16[16,768]{1,0:T(8,128)(2,1)S(1)}, u32[]{:S(2)}, u32[]{:S(2)}) collective-permute-start(bf16[16,768]{1,0:T(8,128)(2,1)S(1)} %get-tuple-element.111.refs_2_.refs_1_), channel_id=1, source_target_pairs={{0,2},{2,0},{4,6},{6,4},{8,10},{10,8},{12,14},{14,12},{16,18},{18,... | collective-permute-start | bytes 73736 | tf_op jit(solution)/shard_map/ppermute | solution.py:785
  73.0 6.1 %collective-permute-start.12 = (bf16[64,768]{1,0:T(8,128)(2,1)S(1)}, bf16[64,768]{1,0:T(8,128)(2,1)S(1)}, u32[]{:S(2)}, u32[]{:S(2)}) collective-permute-start(bf16[64,768]{1,0:T(8,128)(2,1)S(1)} %stage.29.refs_1_.refs_5_), channel_id=1, source_target_pairs={{0,8},{2,10},{4,12},{6,14},{8,0},{10,2},{12,4},{14,6},{16,24},{18,... | collective-permute-start | bytes 294920 | tf_op jit(solution)/shard_map/ppermute | solution.py:785
  75.4 9.0 %collective-permute-start.13 = (bf16[64,768]{1,0:T(8,128)(2,1)S(1)}, bf16[64,768]{1,0:T(8,128)(2,1)S(1)}, u32[]{:S(2)}, u32[]{:S(2)}) collective-permute-start(bf16[64,768]{1,0:T(8,128)(2,1)S(1)} %stage.29.refs_1_.refs_5_), channel_id=1, source_target_pairs={{0,16},{2,18},{4,20},{6,22},{8,24},{10,26},{12,28},{14,30},{16,0},... | collective-permute-start | bytes 294920 | tf_op jit(solution)/shard_map/ppermute | solution.py:785
  77.2 7.2 %collective-permute-start.14 = (bf16[64,768]{1,0:T(8,128)(2,1)S(1)}, bf16[64,768]{1,0:T(8,128)(2,1)S(1)}, u32[]{:S(2)}, u32[]{:S(2)}) collective-permute-start(bf16[64,768]{1,0:T(8,128)(2,1)S(1)} %stage.29.refs_1_.refs_5_), channel_id=1, source_target_pairs={{0,24},{2,26},{4,28},{6,30},{8,16},{10,18},{12,20},{14,22},{16,8},... | collective-permute-start | bytes 294920 | tf_op jit(solution)/shard_map/ppermute | solution.py:785
  77.8 7.9 %collective-permute-start.16 = (bf16[384,768]{1,0:T(8,128)(2,1)}, bf16[384,768]{1,0:T(8,128)(2,1)}, u32[]{:S(2)}, u32[]{:S(2)}) collective-permute-start(bf16[384,768]{1,0:T(8,128)(2,1)} %refs_4_.2), channel_id=1, source_target_pairs={{0,1},{1,0},{2,3},{3,2},{4,5},{5,4},{6,7},{7,6},{8,9},{9,8},{10,11... | collective-permute-start | bytes 1769480 | tf_op jit(solution)/shard_map/ppermute | solution.py:781
  84.5 9.0 %collective-permute-start.17 = (bf16[1024,384]{1,0:T(8,128)(2,1)S(1)}, bf16[1024,384]{1,0:T(8,128)(2,1)}, u32[]{:S(2)}, u32[]{:S(2)}) collective-permute-start(bf16[1024,384]{1,0:T(8,128)(2,1)S(1)} %their_rows.5.refs_5_), channel_id=1, source_target_pairs={{0,1},{1,0},{2,3},{3,2},{4,5},{5,4},{6,7},{7,6},{8,9},{9,8},{10,11... | collective-permute-start | bytes 2359304 | tf_op jit(solution)/shard_map/ppermute | solution.py:781
  102.8 11.2 %collective-permute-start.19 = (bf16[1536,768]{1,0:T(8,128)(2,1)S(1)}, bf16[1536,768]{1,0:T(8,128)(2,1)S(1)}, u32[]{:S(2)}, u32[]{:S(2)}) collective-permute-start(bf16[1536,768]{1,0:T(8,128)(2,1)S(1)} %get-tuple-element.124), channel_id=1, source_target_pairs={{0,1},{1,0},{2,3},{3,2},{4,5},{5,4},{6,7},{7,6},{8,9},{9,8},{10,11... | collective-permute-start | bytes 7077896 | tf_op jit(solution)/shard_map/ppermute | solution.py:781
  113.6 7.6 %collective-permute-start.18 = (bf16[768,1536]{1,0:T(8,128)(2,1)S(1)}, bf16[768,1536]{1,0:T(8,128)(2,1)S(1)}, u32[]{:S(2)}, u32[]{:S(2)}) collective-permute-start(bf16[768,1536]{1,0:T(8,128)(2,1)S(1)} %get-tuple-element.123), channel_id=1, source_target_pairs={{0,1},{1,0},{2,3},{3,2},{4,5},{5,4},{6,7},{7,6},{8,9},{9,8},{10,11... | collective-permute-start | bytes 7077896 | tf_op jit(solution)/shard_map/ppermute | solution.py:781
  120.5 28.1 %collective-permute-start.20 = (bf16[768,768]{1,0:T(8,128)(2,1)S(1)}, bf16[768,768]{1,0:T(8,128)(2,1)S(1)}, u32[]{:S(2)}, u32[]{:S(2)}) collective-permute-start(bf16[768,768]{1,0:T(8,128)(2,1)S(1)} %get-tuple-element.133), channel_id=1, source_target_pairs={{0,2},{2,0},{4,6},{6,4},{8,10},{10,8},{12,14},{14,12},{16,18},{18,... | collective-permute-start | bytes 3538952 | tf_op jit(solution)/shard_map/ppermute | solution.py:785
  133.8 37.6 %collective-permute-start.22 = (bf16[384,1536]{1,0:T(8,128)(2,1)S(1)}, bf16[384,1536]{1,0:T(8,128)(2,1)S(1)}, u32[]{:S(2)}, u32[]{:S(2)}) collective-permute-start(bf16[384,1536]{1,0:T(8,128)(2,1)S(1)} %get-tuple-element.141), channel_id=1, source_target_pairs={{0,4},{2,6},{4,0},{6,2},{8,12},{10,14},{12,8},{14,10},{16,20},{18,... | collective-permute-start | bytes 3538952 | tf_op jit(solution)/shard_map/ppermute | solution.py:785
  149.1 25.3 %collective-permute-start.21 = (bf16[384,768]{1,0:T(8,128)(2,1)S(1)}, bf16[384,768]{1,0:T(8,128)(2,1)S(1)}, u32[]{:S(2)}, u32[]{:S(2)}) collective-permute-start(bf16[384,768]{1,0:T(8,128)(2,1)S(1)} %get-tuple-element.139), channel_id=1, source_target_pairs={{0,4},{2,6},{4,0},{6,2},{8,12},{10,14},{12,8},{14,10},{16,20},{18,... | collective-permute-start | bytes 1769480 | tf_op jit(solution)/shard_map/ppermute | solution.py:785
  185.6 16.2 %collective-permute-start.26 = (bf16[768,384]{1,0:T(8,128)(2,1)S(1)}, bf16[768,384]{1,0:T(8,128)(2,1)S(1)}, u32[]{:S(2)}, u32[]{:S(2)}) collective-permute-start(bf16[768,384]{1,0:T(8,128)(2,1)S(1)} %get-tuple-element.150), channel_id=1, source_target_pairs={{0,2},{2,0},{4,6},{6,4},{8,10},{10,8},{12,14},{14,12},{16,18},{18,... | collective-permute-start | bytes 1769480 | tf_op jit(solution)/shard_map/ppermute | solution.py:785
  187.0 26.7 %collective-permute-start.42 = (bf16[192,1536]{1,0:T(8,128)(2,1)S(1)}, bf16[192,1536]{1,0:T(8,128)(2,1)S(1)}, u32[]{:S(2)}, u32[]{:S(2)}) collective-permute-start(bf16[192,1536]{1,0:T(8,128)(2,1)S(1)} %get-tuple-element.169), channel_id=1, source_target_pairs={{0,2},{2,0},{4,6},{6,4},{8,10},{10,8},{12,14},{14,12},{16,18},{18,... | collective-permute-start | bytes 1769480 | tf_op jit(solution)/shard_map/ppermute | solution.py:785
  187.7 16.2 %collective-permute-start.49 = (bf16[192,768]{1,0:T(8,128)(2,1)S(1)}, bf16[192,768]{1,0:T(8,128)(2,1)S(1)}, u32[]{:S(2)}, u32[]{:S(2)}) collective-permute-start(bf16[192,768]{1,0:T(8,128)(2,1)S(1)} %get-tuple-element.174), channel_id=1, source_target_pairs={{0,8},{2,10},{4,12},{6,14},{8,0},{10,2},{12,4},{14,6},{16,24},{18,... | collective-permute-start | bytes 884744 | tf_op jit(solution)/shard_map/ppermute | solution.py:785
  189.3 26.3 %collective-permute-start.34 = (bf16[832,384]{1,0:T(8,128)(2,1)S(1)}, bf16[832,384]{1,0:T(8,128)(2,1)S(1)}, u32[]{:S(2)}, u32[]{:S(2)}) collective-permute-start(bf16[832,384]{1,0:T(8,128)(2,1)S(1)} %get-tuple-element.158), channel_id=1, source_target_pairs={{0,4},{2,6},{4,0},{6,2},{8,12},{10,14},{12,8},{14,10},{16,20},{18,... | collective-permute-start | bytes 1916936 | tf_op jit(solution)/shard_map/ppermute | solution.py:785
  199.9 98.9 %collective-permute-start.25 = (f32[1024,384]{1,0:T(8,128)}, f32[1024,384]{1,0:T(8,128)}, u32[]{:S(2)}, u32[]{:S(2)}) collective-permute-start(f32[1024,384]{1,0:T(8,128)} %get-tuple-element.149), channel_id=1, source_target_pairs={{0,1},{1,0},{2,3},{3,2},{4,5},{5,4},{6,7},{7,6},{8,9},{9,8},{10,11... | collective-permute-start | bytes 4718600 | tf_op jit(solution)/shard_map/ppermute | solution.py:781
  202.1 16.7 %collective-permute-start.27 = (bf16[384,384]{1,0:T(8,128)(2,1)S(1)}, bf16[384,384]{1,0:T(8,128)(2,1)S(1)}, u32[]{:S(2)}, u32[]{:S(2)}) collective-permute-start(bf16[384,384]{1,0:T(8,128)(2,1)S(1)} %get-tuple-element.152), channel_id=1, source_target_pairs={{0,4},{2,6},{4,0},{6,2},{8,12},{10,14},{12,8},{14,10},{16,20},{18,... | collective-permute-start | bytes 884744 | tf_op jit(solution)/shard_map/ppermute | solution.py:785
  204.1 13.2 %collective-permute-start.50 = (bf16[96,768]{1,0:T(8,128)(2,1)S(1)}, bf16[96,768]{1,0:T(8,128)(2,1)S(1)}, u32[]{:S(2)}, u32[]{:S(2)}) collective-permute-start(bf16[96,768]{1,0:T(8,128)(2,1)S(1)} %get-tuple-element.176), channel_id=1, source_target_pairs={{0,16},{2,18},{4,20},{6,22},{8,24},{10,26},{12,28},{14,30},{16,0},... | collective-permute-start | bytes 442376 | tf_op jit(solution)/shard_map/ppermute | solution.py:785
  214.0 13.6 %collective-permute-start.43 = (bf16[96,1536]{1,0:T(8,128)(2,1)S(1)}, bf16[96,1536]{1,0:T(8,128)(2,1)S(1)}, u32[]{:S(2)}, u32[]{:S(2)}) collective-permute-start(bf16[96,1536]{1,0:T(8,128)(2,1)S(1)} %get-tuple-element.171), channel_id=1, source_target_pairs={{0,8},{2,10},{4,12},{6,14},{8,0},{10,2},{12,4},{14,6},{16,24},{18,... | collective-permute-start | bytes 884744 | tf_op jit(solution)/shard_map/ppermute | solution.py:785
  215.9 15.5 %collective-permute-start.35 = (bf16[416,384]{1,0:T(8,128)(2,1)S(1)}, bf16[416,384]{1,0:T(8,128)(2,1)S(1)}, u32[]{:S(2)}, u32[]{:S(2)}) collective-permute-start(bf16[416,384]{1,0:T(8,128)(2,1)S(1)} %get-tuple-element.160), channel_id=1, source_target_pairs={{0,2},{2,0},{4,6},{6,4},{8,10},{10,8},{12,14},{14,12},{16,18},{18,... | collective-permute-start | bytes 958472 | tf_op jit(solution)/shard_map/ppermute | solution.py:785
  217.3 11.0 %collective-permute-start.51 = (bf16[96,768]{1,0:T(8,128)(2,1)S(1)}, bf16[96,768]{1,0:T(8,128)(2,1)S(1)}, u32[]{:S(2)}, u32[]{:S(2)}) collective-permute-start(bf16[96,768]{1,0:T(8,128)(2,1)S(1)} %stage.54.refs_1_), channel_id=1, source_target_pairs={{0,16},{2,18},{4,20},{6,22},{8,24},{10,26},{12,28},{14,30},{16,0},... | collective-permute-start | bytes 442376 | tf_op jit(solution)/shard_map/ppermute | solution.py:785
  218.9 14.2 %collective-permute-start.28 = (bf16[192,384]{1,0:T(8,128)(2,1)S(1)}, bf16[192,384]{1,0:T(8,128)(2,1)S(1)}, u32[]{:S(2)}, u32[]{:S(2)}) collective-permute-start(bf16[192,384]{1,0:T(8,128)(2,1)S(1)} %get-tuple-element.154), channel_id=1, source_target_pairs={{0,8},{2,10},{4,12},{6,14},{8,0},{10,2},{12,4},{14,6},{16,24},{18,... | collective-permute-start | bytes 442376 | tf_op jit(solution)/shard_map/ppermute | solution.py:785
  227.7 8.6 %collective-permute-start.44 = (bf16[48,1536]{1,0:T(8,128)(2,1)S(1)}, bf16[48,1536]{1,0:T(8,128)(2,1)S(1)}, u32[]{:S(2)}, u32[]{:S(2)}) collective-permute-start(bf16[48,1536]{1,0:T(8,128)(2,1)S(1)} %get-tuple-element.173), channel_id=1, source_target_pairs={{0,16},{2,18},{4,20},{6,22},{8,24},{10,26},{12,28},{14,30},{16,0},... | collective-permute-start | bytes 442376 | tf_op jit(solution)/shard_map/ppermute | solution.py:785
  228.4 26.8 %collective-permute-start.52 = (bf16[192,768]{1,0:T(8,128)(2,1)S(1)}, bf16[192,768]{1,0:T(8,128)(2,1)S(1)}, u32[]{:S(2)}, u32[]{:S(2)}) collective-permute-start(bf16[192,768]{1,0:T(8,128)(2,1)S(1)} %stage.55.refs_1_), channel_id=1, source_target_pairs={{0,8},{2,10},{4,12},{6,14},{8,0},{10,2},{12,4},{14,6},{16,24},{18,... | collective-permute-start | bytes 884744 | tf_op jit(solution)/shard_map/ppermute | solution.py:785
  231.6 15.8 %collective-permute-start.36 = (bf16[208,384]{1,0:T(8,128)(2,1)S(1)}, bf16[208,384]{1,0:T(8,128)(2,1)S(1)}, u32[]{:S(2)}, u32[]{:S(2)}) collective-permute-start(bf16[208,384]{1,0:T(8,128)(2,1)S(1)} %get-tuple-element.162), channel_id=1, source_target_pairs={{0,8},{2,10},{4,12},{6,14},{8,0},{10,2},{12,4},{14,6},{16,24},{18,... | collective-permute-start | bytes 479240 | tf_op jit(solution)/shard_map/ppermute | solution.py:785
  233.2 10.6 %collective-permute-start.29 = (bf16[96,384]{1,0:T(8,128)(2,1)S(1)}, bf16[96,384]{1,0:T(8,128)(2,1)S(1)}, u32[]{:S(2)}, u32[]{:S(2)}) collective-permute-start(bf16[96,384]{1,0:T(8,128)(2,1)S(1)} %get-tuple-element.156), channel_id=1, source_target_pairs={{0,16},{2,18},{4,20},{6,22},{8,24},{10,26},{12,28},{14,30},{16,0},... | collective-permute-start | bytes 221192 | tf_op jit(solution)/shard_map/ppermute | solution.py:785
  236.3 11.2 %collective-permute-start.45 = (bf16[48,1536]{1,0:T(8,128)(2,1)S(1)}, bf16[48,1536]{1,0:T(8,128)(2,1)S(1)}, u32[]{:S(2)}, u32[]{:S(2)}) collective-permute-start(bf16[48,1536]{1,0:T(8,128)(2,1)S(1)} %stage.49.refs_1_), channel_id=1, source_target_pairs={{0,16},{2,18},{4,20},{6,22},{8,24},{10,26},{12,28},{14,30},{16,0},... | collective-permute-start | bytes 442376 | tf_op jit(solution)/shard_map/ppermute | solution.py:785
  243.8 7.9 %collective-permute-start.30 = (bf16[96,384]{1,0:T(8,128)(2,1)S(1)}, bf16[96,384]{1,0:T(8,128)(2,1)S(1)}, u32[]{:S(2)}, u32[]{:S(2)}) collective-permute-start(bf16[96,384]{1,0:T(8,128)(2,1)S(1)} %stage.36.refs_1_), channel_id=1, source_target_pairs={{0,16},{2,18},{4,20},{6,22},{8,24},{10,26},{12,28},{14,30},{16,0},... | collective-permute-start | bytes 221192 | tf_op jit(solution)/shard_map/ppermute | solution.py:785
  247.4 6.8 %collective-permute-start.37 = (bf16[104,384]{1,0:T(8,128)(2,1)S(1)}, bf16[104,384]{1,0:T(8,128)(2,1)S(1)}, u32[]{:S(2)}, u32[]{:S(2)}) collective-permute-start(bf16[104,384]{1,0:T(8,128)(2,1)S(1)} %get-tuple-element.164), channel_id=1, source_target_pairs={{0,16},{2,18},{4,20},{6,22},{8,24},{10,26},{12,28},{14,30},{16,0},... | collective-permute-start | bytes 239624 | tf_op jit(solution)/shard_map/ppermute | solution.py:785
  247.6 18.3 %collective-permute-start.46 = (bf16[96,1536]{1,0:T(8,128)(2,1)S(1)}, bf16[96,1536]{1,0:T(8,128)(2,1)S(1)}, u32[]{:S(2)}, u32[]{:S(2)}) collective-permute-start(bf16[96,1536]{1,0:T(8,128)(2,1)S(1)} %stage.50.refs_1_), channel_id=1, source_target_pairs={{0,8},{2,10},{4,12},{6,14},{8,0},{10,2},{12,4},{14,6},{16,24},{18,... | collective-permute-start | bytes 884744 | tf_op jit(solution)/shard_map/ppermute | solution.py:785
  251.8 11.6 %collective-permute-start.31 = (bf16[192,384]{1,0:T(8,128)(2,1)S(1)}, bf16[192,384]{1,0:T(8,128)(2,1)S(1)}, u32[]{:S(2)}, u32[]{:S(2)}) collective-permute-start(bf16[192,384]{1,0:T(8,128)(2,1)S(1)} %stage.37.refs_1_), channel_id=1, source_target_pairs={{0,8},{2,10},{4,12},{6,14},{8,0},{10,2},{12,4},{14,6},{16,24},{18,... | collective-permute-start | bytes 442376 | tf_op jit(solution)/shard_map/ppermute | solution.py:785
  254.2 6.0 %collective-permute-start.38 = (bf16[104,384]{1,0:T(8,128)(2,1)S(1)}, bf16[104,384]{1,0:T(8,128)(2,1)S(1)}, u32[]{:S(2)}, u32[]{:S(2)}) collective-permute-start(bf16[104,384]{1,0:T(8,128)(2,1)S(1)} %stage.43.refs_1_), channel_id=1, source_target_pairs={{0,16},{2,18},{4,20},{6,22},{8,24},{10,26},{12,28},{14,30},{16,0},... | collective-permute-start | bytes 239624 | tf_op jit(solution)/shard_map/ppermute | solution.py:785
  255.3 22.4 %collective-permute-start.53 = (bf16[384,768]{1,0:T(8,128)(2,1)S(1)}, bf16[384,768]{1,0:T(8,128)(2,1)S(1)}, u32[]{:S(2)}, u32[]{:S(2)}) collective-permute-start(bf16[384,768]{1,0:T(8,128)(2,1)S(1)} %stage.56.refs_1_), channel_id=1, source_target_pairs={{0,4},{2,6},{4,0},{6,2},{8,12},{10,14},{12,8},{14,10},{16,20},{18,... | collective-permute-start | bytes 1769480 | tf_op jit(solution)/shard_map/ppermute | solution.py:785
  260.3 6.3 %collective-permute-start.39 = (bf16[208,384]{1,0:T(8,128)(2,1)S(1)}, bf16[208,384]{1,0:T(8,128)(2,1)S(1)}, u32[]{:S(2)}, u32[]{:S(2)}) collective-permute-start(bf16[208,384]{1,0:T(8,128)(2,1)S(1)} %stage.44.refs_1_), channel_id=1, source_target_pairs={{0,8},{2,10},{4,12},{6,14},{8,0},{10,2},{12,4},{14,6},{16,24},{18,... | collective-permute-start | bytes 479240 | tf_op jit(solution)/shard_map/ppermute | solution.py:785
  263.5 12.1 %collective-permute-start.32 = (bf16[384,384]{1,0:T(8,128)(2,1)S(1)}, bf16[384,384]{1,0:T(8,128)(2,1)S(1)}, u32[]{:S(2)}, u32[]{:S(2)}) collective-permute-start(bf16[384,384]{1,0:T(8,128)(2,1)S(1)} %stage.38.refs_1_), channel_id=1, source_target_pairs={{0,4},{2,6},{4,0},{6,2},{8,12},{10,14},{12,8},{14,10},{16,20},{18,... | collective-permute-start | bytes 884744 | tf_op jit(solution)/shard_map/ppermute | solution.py:785
  266.0 21.5 %collective-permute-start.47 = (bf16[192,1536]{1,0:T(8,128)(2,1)S(1)}, bf16[192,1536]{1,0:T(8,128)(2,1)S(1)}, u32[]{:S(2)}, u32[]{:S(2)}) collective-permute-start(bf16[192,1536]{1,0:T(8,128)(2,1)S(1)} %stage.51.refs_1_), channel_id=1, source_target_pairs={{0,2},{2,0},{4,6},{6,4},{8,10},{10,8},{12,14},{14,12},{16,18},{18,... | collective-permute-start | bytes 1769480 | tf_op jit(solution)/shard_map/ppermute | solution.py:785
  266.5 27.2 %collective-permute-start.8 = (bf16[1024,384]{1,0:T(8,128)(2,1)}, bf16[1024,384]{1,0:T(8,128)(2,1)}, u32[]{:S(2)}, u32[]{:S(2)}) collective-permute-start(bf16[1024,384]{1,0:T(8,128)(2,1)} %get-tuple-element.110), channel_id=1, source_target_pairs={{0,1},{1,0},{2,3},{3,2},{4,5},{5,4},{6,7},{7,6},{8,9},{9,8},{10,11... | collective-permute-start | bytes 2359304 | tf_op jit(solution)/shard_map/ppermute | solution.py:781
  275.6 11.8 %collective-permute-start.40 = (bf16[416,384]{1,0:T(8,128)(2,1)S(1)}, bf16[416,384]{1,0:T(8,128)(2,1)S(1)}, u32[]{:S(2)}, u32[]{:S(2)}) collective-permute-start(bf16[416,384]{1,0:T(8,128)(2,1)S(1)} %stage.45.refs_1_), channel_id=1, source_target_pairs={{0,2},{2,0},{4,6},{6,4},{8,10},{10,8},{12,14},{14,12},{16,18},{18,... | collective-permute-start | bytes 958472 | tf_op jit(solution)/shard_map/ppermute | solution.py:785
  277.8 25.9 %collective-permute-start.33 = (bf16[768,384]{1,0:T(8,128)(2,1)}, bf16[768,384]{1,0:T(8,128)(2,1)}, u32[]{:S(2)}, u32[]{:S(2)}) collective-permute-start(bf16[768,384]{1,0:T(8,128)(2,1)} %stage.39.refs_1_), channel_id=1, source_target_pairs={{0,2},{2,0},{4,6},{6,4},{8,10},{10,8},{12,14},{14,12},{16,18},{18,... | collective-permute-start | bytes 1769480 | tf_op jit(solution)/shard_map/ppermute | solution.py:785
  287.4 35.6 %collective-permute-start.54 = (bf16[768,768]{1,0:T(8,128)(2,1)S(1)}, bf16[768,768]{1,0:T(8,128)(2,1)S(1)}, u32[]{:S(2)}, u32[]{:S(2)}) collective-permute-start(bf16[768,768]{1,0:T(8,128)(2,1)S(1)} %stage.57.refs_1_), channel_id=1, source_target_pairs={{0,2},{2,0},{4,6},{6,4},{8,10},{10,8},{12,14},{14,12},{16,18},{18,... | collective-permute-start | bytes 3538952 | tf_op jit(solution)/shard_map/ppermute | solution.py:785
  288.3 17.4 %collective-permute-start.41 = (bf16[832,384]{1,0:T(8,128)(2,1)S(1)}, bf16[832,384]{1,0:T(8,128)(2,1)}, u32[]{:S(2)}, u32[]{:S(2)}) collective-permute-start(bf16[832,384]{1,0:T(8,128)(2,1)S(1)} %stage.46.refs_3_), channel_id=1, source_target_pairs={{0,4},{2,6},{4,0},{6,2},{8,12},{10,14},{12,8},{14,10},{16,20},{18,... | collective-permute-start | bytes 1916936 | tf_op jit(solution)/shard_map/ppermute | solution.py:785
  293.7 32.3 %collective-permute-start.48 = (bf16[384,1536]{1,0:T(8,128)(2,1)}, bf16[384,1536]{1,0:T(8,128)(2,1)}, u32[]{:S(2)}, u32[]{:S(2)}) collective-permute-start(bf16[384,1536]{1,0:T(8,128)(2,1)} %stage.52.refs_1_), channel_id=1, source_target_pairs={{0,4},{2,6},{4,0},{6,2},{8,12},{10,14},{12,8},{14,10},{16,20},{18,... | collective-permute-start | bytes 3538952 | tf_op jit(solution)/shard_map/ppermute | solution.py:785
  (57 other events, 298.7 us)
